TPU v7x, 32 devices: a whole 2x2x4 slice. The times are simulated.
32 devices in a mesh: grp: 4 (over z), sp: 8 (over y, x, core).
Axes of the slice: x: 2, y: 2, z: 4, core: 2. Of those that a mesh axis runs over, the one named last changes fastest.
Arguments:
- tokens: bfloat16 [4096, 2880], P(('grp', 'sp')), may hold values from -6 to 6
- d_output: bfloat16 [4096, 2880], P(('grp', 'sp')), may hold values from -6 to 6
- expert_ids: int32 [4096, 2], P(('grp', 'sp')), may hold values from 0 to 63, all different within a row; in each aligned block of 128 rows (0 to 127, 128 to 255, ...) at most 8 rows name the same one
- route_weight: float32 [4096, 2], P(('grp', 'sp')), may hold values from 0.2 to 1
- gate_codes: bfloat16 [128, 2880, 720], P(('grp', 'sp')), may hold values from -1 to 1, as said below
- up_codes: bfloat16 [128, 2880, 720], P(('grp', 'sp')), may hold values from -1 to 1, as said below
- down_codes: bfloat16 [128, 720, 2880], P(('grp', 'sp')), may hold values from -1 to 1, as said below
- code_scales: float32 [64, 3], replicated, may hold values from 0.015 to 0.045
Outputs:
- output: bfloat16 [4096, 2880], P(('grp', 'sp'))
- d_tokens: bfloat16 [4096, 2880], P(('grp', 'sp'))
- d_route: float32 [4096, 2], P(('grp', 'sp'))
Inputs may be any that keep to these rules, and one draw needn't show every extreme that they name: `expert_ids`: among the 128 x 2 entries of one device's tokens no expert appears more than 8 times, and some expert appears exactly 8 times; a token names 2 different experts. `gate_codes`: every entry is -1, 0 or 1. `up_codes`: every entry is -1, 0 or 1. `down_codes`: every entry is -1, 0 or 1.
All inputs are finite; a program needn't handle non-finite values.
Results may differ from a plain program's by a relative error of at most 0.0065.
Values may be sent and summed in bfloat16 or wider, within the bound.
No kernel may reach another device: no remote copies, remote signals or barrier semaphores. Data moves between devices by JAX's collectives and lax.ppermute only.
A program may use at most 192 MiB of HBM per device.

v0:
```python
import jax
import jax.numpy as jnp
from jax import lax
from jax.sharding import PartitionSpec as P


def silu_parts(gate_value):
    sigmoid_gate = 1.0 / (1.0 + jnp.exp(-gate_value))
    return (sigmoid_gate, gate_value * sigmoid_gate)


def per_device(
    tokens, d_output, expert_ids, route_weight, gate_codes, up_codes, down_codes, code_scales
):
    tok_rows, width = tokens.shape
    top_count = expert_ids.shape[1]
    shards_here = gate_codes.shape[0]
    expert_count = code_scales.shape[0]
    group_count = lax.axis_size("grp")
    inner_count = lax.axis_size("sp")
    device_count = group_count * inner_count
    slot_count = 2 * tok_rows * top_count // expert_count
    flat_ids = expert_ids.reshape(-1)
    labels = jnp.arange(expert_count, dtype=jnp.int32)
    onehot = (flat_ids[:, None] == labels[None, :]).astype(jnp.int32)
    slot_rank = jnp.sum((jnp.cumsum(onehot, axis=0) - onehot) * onehot, axis=1)
    target = flat_ids * slot_count + slot_rank
    cells = jnp.arange(expert_count * slot_count, dtype=jnp.int32)
    placing = (target[:, None] == cells[None, :]).astype(jnp.bfloat16)
    token_rows = jnp.repeat(tokens, top_count, axis=0)
    grad_rows = jnp.repeat(d_output, top_count, axis=0).astype(jnp.float32)
    scaled = (route_weight.reshape(-1)[:, None] * grad_rows).astype(jnp.bfloat16)
    payload = jnp.concatenate([token_rows, scaled], axis=1)
    arranged = lax.dot_general(
        placing, payload, (((0,), (0,)), ((), ())), preferred_element_type=jnp.float32
    )
    arranged = arranged.astype(jnp.bfloat16).reshape(expert_count, slot_count, 2 * width)
    arranged = jnp.concatenate([arranged, arranged], axis=0)
    rows_out = arranged[:, :, :width]
    grads_out = arranged[:, :, width:]
    direct_shape = (device_count, shards_here, slot_count, width)
    rows_in, grads_in = (
        lax.all_to_all(
            rows_out.reshape(direct_shape), ("grp", "sp"), split_axis=0, concat_axis=0, tiled=True
        ),
        lax.all_to_all(
            grads_out.reshape(direct_shape), ("grp", "sp"), split_axis=0, concat_axis=0, tiled=True
        ),
    )
    device_index = lax.axis_index("grp") * inner_count + lax.axis_index("sp")
    first_shard = device_index * shards_here
    scales_here = lax.dynamic_slice_in_dim(code_scales, first_shard % expert_count, shards_here, 0)
    scale_gate = scales_here[:, 0][None, :, None, None]
    scale_up = scales_here[:, 1][None, :, None, None]
    scale_down = scales_here[:, 2][None, :, None, None]
    gate_value = (
        jnp.einsum("nicd,idh->nich", rows_in, gate_codes, preferred_element_type=jnp.float32)
        * scale_gate
    )
    up_value = (
        jnp.einsum("nicd,idh->nich", rows_in, up_codes, preferred_element_type=jnp.float32)
        * scale_up
    )
    sigmoid_gate, silu_gate = silu_parts(gate_value)
    activation = (silu_gate * up_value).astype(jnp.bfloat16)
    expert_part = (
        jnp.einsum("nich,ihd->nicd", activation, down_codes, preferred_element_type=jnp.float32)
        * scale_down
    )
    grad_activation = (
        jnp.einsum("nicd,ihd->nich", grads_in, down_codes, preferred_element_type=jnp.float32)
        * scale_down
    )
    grad_gate = (
        grad_activation * up_value * sigmoid_gate * (1.0 + gate_value * (1.0 - sigmoid_gate))
    ).astype(jnp.bfloat16)
    grad_up = (grad_activation * silu_gate).astype(jnp.bfloat16)
    grad_part = (
        jnp.einsum("nich,idh->nicd", grad_gate, gate_codes, preferred_element_type=jnp.float32)
        * scale_gate
    )
    grad_part = (
        grad_part
        + jnp.einsum("nich,idh->nicd", grad_up, up_codes, preferred_element_type=jnp.float32)
        * scale_up
    )
    returned_part, returned_grad = (
        lax.all_to_all(expert_part, ("grp", "sp"), split_axis=0, concat_axis=0, tiled=True),
        lax.all_to_all(grad_part, ("grp", "sp"), split_axis=0, concat_axis=0, tiled=True),
    )
    returned_part = returned_part.reshape(2 * expert_count, slot_count, width)
    returned_grad = returned_grad.reshape(2 * expert_count, slot_count, width)
    expert_out = (returned_part[:expert_count] + returned_part[expert_count:]).astype(jnp.bfloat16)
    expert_grad = (returned_grad[:expert_count] + returned_grad[expert_count:]).astype(jnp.bfloat16)
    gathered = jnp.concatenate(
        [expert_out.reshape(-1, width), expert_grad.reshape(-1, width)], axis=1
    )
    picked = jnp.dot(placing, gathered, preferred_element_type=jnp.float32)
    picked_out = picked[:, :width].reshape(tok_rows, top_count, width)
    picked_grad = picked[:, width:].reshape(tok_rows, top_count, width)
    output = jnp.sum(route_weight[:, :, None] * picked_out, axis=1).astype(jnp.bfloat16)
    d_route = jnp.sum(d_output.astype(jnp.float32)[:, None, :] * picked_out, axis=2)
    d_tokens = jnp.sum(picked_grad, axis=1).astype(jnp.bfloat16)
    return (output, d_tokens, d_route)


def solution(mesh):
    return jax.shard_map(
        per_device,
        mesh=mesh,
        in_specs=(
            P(("grp", "sp"), None),
            P(("grp", "sp"), None),
            P(("grp", "sp"), None),
            P(("grp", "sp"), None),
            P(("grp", "sp"), None, None),
            P(("grp", "sp"), None, None),
            P(("grp", "sp"), None, None),
            P(),
        ),
        out_specs=(P(("grp", "sp"), None), P(("grp", "sp"), None), P(("grp", "sp"), None)),
        check_vma=False,
    )
```

profile of v0, /device:TPU:0, one launch (start us, length us, event | category | flops | bytes accessed | tf_op | source)
XLA Modules:
  0.0 958.7 jit_solution(18281871637539441224)
XLA Ops:
  0.6 0.0 copy-start
  0.6 0.8 copy.27
  1.4 0.1 reshape.78
  1.6 0.1 eq.41
  1.7 1.4 copy.32
  3.1 2.6 broadcast_in_dim.5
  5.8 3.7 convert_element_type.54
  9.5 0.1 copy.26
  9.6 0.1 mul.137
  9.8 2.3 copy.30
  12.0 3.1 broadcast_in_dim.4
  15.1 4.4 reshape.80
  19.5 0.6 reduce-window.6
  20.1 0.2 slice_reduce_fusion
  20.4 0.1 fusion.52
  20.5 0.3 multiply_convert_fusion
  20.8 1.0 copy-done.2
  21.7 1.9 fusion.12
  23.7 14.5 %fusion.17 = (bf16[128,8,2880]{2,1,0:T(8,128)(2,1)}, bf16[128,8,2880]{2,1,0:T(8,128)(2,1)S(1)}) fusion(bf16[64,8,5760]{2,1,0:T(8,128)(2,1)S(1)} %fusion.12), kind=kLoop, calls=%fused_computation.18 | loop fusion | flops 23592960 | bytes 17694720 | tf_op jit(solution)/shard_map/concatenate | solution.py:38
  38.2 140.2 %all_to_all.20 = bf16[32,4,8,2880]{3,2,1,0:T(8,128)(2,1)} all-to-all(bf16[32,4,8,2880]{3,2,1,0:T(8,128)(2,1)S(1)} %bitcast.106), channel_id=1, replica_groups=mesh['grp'=4,'sp'=8] {'grp','sp'}, dimensions={0} | all-to-all | bytes 11796480 | tf_op jit(solution)/shard_map/all_to_all | solution.py:46
  178.4 4.1 all-to-all-start
  182.5 0.1 constant_dynamic-slice_fusion
  182.6 11.4 %fusion.8 = f32[4,32,8,720]{3,2,1,0:T(8,128)} fusion(bf16[4,720,2880]{2,1,0:T(8,128)(2,1)} %param.14, bf16[32,4,8,2880]{3,2,1,0:T(8,128)(2,1)} %all_to_all.20), kind=kOutput, calls=%fused_computation.8 | convolution fusion | flops 4246732800 | bytes 25436160 | tf_op jit(solution)/shard_map/nicd,ihd->nich/dot_general | solution.py:71
  194.0 122.7 %all-to-all-done = bf16[32,4,8,2880]{3,2,1,0:T(8,128)(2,1)} async-done(((bf16[32,4,8,2880]{3,2,1,0:T(8,128)(2,1)}), bf16[32,4,8,2880]{3,2,1,0:T(8,128)(2,1)}, u32[]{:S(2)}, u32[]{:S(2)}) %all-to-all-start) | async-done | bytes 5898272 | tf_op jit(solution)/shard_map/all_to_all | solution.py:43
  316.6 10.6 %fusion.6 = f32[4,32,8,720]{3,2,1,0:T(8,128)S(1)} fusion(bf16[4,2880,720]{1,2,0:T(8,128)(2,1)} %param.12, bf16[32,4,8,2880]{3,2,1,0:T(8,128)(2,1)} %all-to-all-done), kind=kOutput, calls=%fused_computation.6 | convolution fusion | flops 4246732800 | bytes 25436160 | tf_op jit(solution)/shard_map/nicd,idh->nich/dot_general | solution.py:57
  327.2 15.6 %fusion = f32[4,32,8,2880]{3,2,1,0:T(8,128)} fusion(bf16[4,2880,720]{1,2,0:T(8,128)(2,1)} %param.13, f32[4,32,8,720]{3,2,1,0:T(8,128)} %fusion.8, f32[4]{0:T(128)S(1)} %get-tuple-element.15, f32[4,32,8,720]{3,2,1,0:T(8,128)S(1)} %fusion.6, f32[4]{0:T(128)S(1)} %get-tuple-element.16), kind=kOutput, calls=%fused_computation | convolution fusion | flops 4252631040 | bytes 34283552 | tf_op jit(solution)/shard_map/nich,idh->nicd/dot_general | solution.py:84
  342.9 11.5 %fusion.2 = f32[4,32,8,720]{3,2,1,0:T(8,128)} fusion(bf16[4,2880,720]{1,2,0:T(8,128)(2,1)} %param.13, bf16[32,4,8,2880]{3,2,1,0:T(8,128)(2,1)} %all-to-all-done), kind=kOutput, calls=%fused_computation.2 | convolution fusion | flops 4246732800 | bytes 25436160 | tf_op jit(solution)/shard_map/nicd,idh->nich/dot_general | solution.py:61
  354.4 18.2 %add_bitcast_fusion = f32[32,4,8,2880]{3,2,0,1:T(8,128)} fusion(f32[4,32,8,2880]{3,2,1,0:T(8,128)} %fusion, bf16[4,2880,720]{1,2,0:T(8,128)(2,1)} %param.12, f32[4]{0:T(128)S(1)} %get-tuple-element.14, f32[4]{0:T(128)S(1)} %get-tuple-element.16, f32[4,32,8,720]{3,2,1,0:T(8,128)} %fusion.8, f32[4,32,8,720]{3,2,1,0:T(8,128)} %fusion.2, ...), kind=kOutput, calls=%fused_computation.12 | convolution fusion | flops 4265164800 | bytes 49029168 | tf_op jit(solution)/shard_map/nich,idh->nicd/dot_general | solution.py:79
  372.6 10.3 %copy.37 = f32[32,4,8,2880]{3,2,1,0:T(8,128)} copy(f32[32,4,8,2880]{3,2,0,1:T(8,128)} %add_bitcast_fusion) | data formatting | bytes 23592960 | tf_op jit(solution)/shard_map/add | solution.py:83
  382.9 3.7 all-to-all-start.3
  386.7 14.9 %multiply_bitcast_fusion = f32[32,4,8,2880]{3,2,0,1:T(8,128)} fusion(bf16[4,720,2880]{2,1,0:T(8,128)(2,1)} %param.14, f32[4]{0:T(128)S(1)} %get-tuple-element.15, f32[4,32,8,720]{3,2,1,0:T(8,128)} %fusion.2, f32[4]{0:T(128)S(1)} %get-tuple-element.14, f32[4,32,8,720]{3,2,1,0:T(8,128)} %copy-done.3, f32[4]{0:T(128)S(1)} %get-tuple-element.16), kind=kOutput, calls=%fused_computation.13 | convolution fusion | flops 4255580160 | bytes 34283568 | tf_op jit(solution)/shard_map/nich,ihd->nicd/dot_general | solution.py:67
  401.6 10.3 %copy.35 = f32[32,4,8,2880]{3,2,1,0:T(8,128)} copy(f32[32,4,8,2880]{3,2,0,1:T(8,128)} %multiply_bitcast_fusion) | data formatting | bytes 23592960 | tf_op jit(solution)/shard_map/mul | solution.py:67
  412.0 241.9 %all-to-all-done.3 = f32[32,4,8,2880]{3,2,1,0:T(8,128)} async-done(((f32[32,4,8,2880]{3,2,1,0:T(8,128)}), f32[32,4,8,2880]{3,2,1,0:T(8,128)}, u32[]{:S(2)}, u32[]{:S(2)}) %all-to-all-start.3) | async-done | bytes 11796512 | tf_op jit(solution)/shard_map/all_to_all | solution.py:89
  653.8 3.9 all-to-all-start.1
  657.8 6.7 fusion.18
  664.5 260.4 %all-to-all-done.1 = f32[32,4,8,2880]{3,2,1,0:T(8,128)} async-done(((f32[32,4,8,2880]{3,2,1,0:T(8,128)}), f32[32,4,8,2880]{3,2,1,0:T(8,128)}, u32[]{:S(2)}, u32[]{:S(2)}) %all-to-all-start.1) | async-done | bytes 11796512 | tf_op jit(solution)/shard_map/all_to_all | solution.py:88
  924.9 5.2 fusion.19
  930.1 0.1 copy-done.4
  930.2 2.0 fusion.21
  932.2 3.5 multiply_reduce_fusion
  935.7 3.5 reshape.84
  939.3 5.2 multiply_reduce_fusion.1
  944.4 2.3 copy.38
  946.7 3.8 reshape.85
  950.5 5.0 reduce_sum.40
  955.5 2.3 copy.39
  957.7 0.1 reduce_sum.42
  957.9 0.6 copy.40
  (14 shorter events, 0.1 us)
Async XLA Ops:
  0.6 181.9 %copy-start = (f32[64,3]{0,1:T(4,128)S(1)}, f32[64,3]{0,1:T(4,128)}, u32[]{:S(2)}) copy-start(f32[64,3]{0,1:T(4,128)} %param.15) | copy-start | bytes 2308
  5.8 3.7 copy-start.5
  20.3 1.4 copy-start.2
  178.4 138.3 %all-to-all-start = ((bf16[32,4,8,2880]{3,2,1,0:T(8,128)(2,1)}), bf16[32,4,8,2880]{3,2,1,0:T(8,128)(2,1)}, u32[]{:S(2)}, u32[]{:S(2)}) async-start(bf16[32,4,8,2880]{3,2,1,0:T(8,128)(2,1)} %bitcast.105), calls=%async_computation | async-start | bytes 12058624 | tf_op jit(solution)/shard_map/all_to_all | solution.py:43
  327.2 15.7 %copy-start.3 = (f32[4,32,8,720]{3,2,1,0:T(8,128)}, f32[4,32,8,720]{3,2,1,0:T(8,128)S(1)}, u32[]{:S(2)}) copy-start(f32[4,32,8,720]{3,2,1,0:T(8,128)S(1)} %fusion.6) | copy-start | bytes 8847364
  382.9 270.9 %all-to-all-start.3 = ((f32[32,4,8,2880]{3,2,1,0:T(8,128)}), f32[32,4,8,2880]{3,2,1,0:T(8,128)}, u32[]{:S(2)}, u32[]{:S(2)}) async-start(f32[32,4,8,2880]{3,2,1,0:T(8,128)} %copy.37), calls=%async_computation.3 | async-start | bytes 24117248 | tf_op jit(solution)/shard_map/all_to_all | solution.py:89
  653.8 271.1 %all-to-all-start.1 = ((f32[32,4,8,2880]{3,2,1,0:T(8,128)}), f32[32,4,8,2880]{3,2,1,0:T(8,128)}, u32[]{:S(2)}, u32[]{:S(2)}) async-start(f32[32,4,8,2880]{3,2,1,0:T(8,128)} %copy.35), calls=%async_computation.1 | async-start | bytes 24117248 | tf_op jit(solution)/shard_map/all_to_all | solution.py:88
  924.9 5.3 copy-start.4
  946.7 11.8 %copy-start.1 = (f32[64,3]{0,1:T(4,128)S(1)}, f32[64,3]{0,1:T(4,128)}, u32[]{:S(2)}) copy-start(f32[64,3]{0,1:T(4,128)} %param.15) | copy-start | bytes 2308
where the time goes:
time: 969 us; the launch traced here: 959 us
  waiting for transfers between devices  625 us (64%)
  blocking collectives  140 us (14%)
  matrix products  86.2 us (9%)
  local copies, waits for them, and re-layouts  53.4 us (6%)
  other arithmetic  41.1 us (4%)
  starting transfers between devices  11.7 us (1%)
    all_to_all x1, waiting for transfers between devices, per_device(): lax.all_to_all(expert_part, ('grp', 'sp'), split_axis=0, concat_axis=0, t...  260 us
    all_to_all x1, waiting for transfers between devices, per_device(): lax.all_to_all(grad_part, ('grp', 'sp'), split_axis=0, concat_axis=0, til...  242 us
    all_to_all x1, blocking collectives, per_device(): lax.all_to_all(grads_out.reshape(direct_shape), ('grp', 'sp'), split_axis...  140 us
    all_to_all x1, waiting for transfers between devices, per_device(): lax.all_to_all(rows_out.reshape(direct_shape), ('grp', 'sp'), split_axis=...  123 us
  transfers between devices with their start and end apart: 3, of which 3 were waited for; matrix products, arithmetic and copies ran while one was open for 5% of the time, Pallas kernels for 0%

commit v1 on v0

v1 whole, which is shorter than its diff:
```python
import functools

import jax
import jax.numpy as jnp
from jax import lax
from jax.experimental import pallas as pl
from jax.experimental.pallas import tpu as pltpu
from jax.sharding import PartitionSpec as P

AXES = ("grp", "sp")
CORE, COL, ROW = 1, 2, 4
VMEM_BYTES = 56 * 1024 * 1024
F32, BF16 = jnp.float32, jnp.bfloat16


def silu_parts(gate_value):
    sigmoid_gate = 1.0 / (1.0 + jnp.exp(-gate_value))
    return (sigmoid_gate, gate_value * sigmoid_gate)


def per_device(
    tokens, d_output, expert_ids, route_weight, gate_codes, up_codes, down_codes, code_scales
):
    tok_rows, width = tokens.shape
    top_count = expert_ids.shape[1]
    shards_here = gate_codes.shape[0]
    expert_count = code_scales.shape[0]
    group_count = lax.axis_size("grp")
    inner_count = lax.axis_size("sp")
    device_count = group_count * inner_count
    slot_count = 2 * tok_rows * top_count // expert_count
    flat_ids = expert_ids.reshape(-1)
    labels = jnp.arange(expert_count, dtype=jnp.int32)
    onehot = (flat_ids[:, None] == labels[None, :]).astype(jnp.int32)
    slot_rank = jnp.sum((jnp.cumsum(onehot, axis=0) - onehot) * onehot, axis=1)
    target = flat_ids * slot_count + slot_rank
    cells = jnp.arange(expert_count * slot_count, dtype=jnp.int32)
    placing = (target[:, None] == cells[None, :]).astype(jnp.bfloat16)
    token_rows = jnp.repeat(tokens, top_count, axis=0)
    grad_rows = jnp.repeat(d_output, top_count, axis=0).astype(jnp.float32)
    scaled = (route_weight.reshape(-1)[:, None] * grad_rows).astype(jnp.bfloat16)
    payload = jnp.concatenate([token_rows, scaled], axis=1)
    arranged = lax.dot_general(
        placing, payload, (((0,), (0,)), ((), ())), preferred_element_type=jnp.float32
    )
    arranged = arranged.astype(jnp.bfloat16).reshape(expert_count, slot_count, 2 * width)
    arranged = jnp.concatenate([arranged, arranged], axis=0)
    rows_out = arranged[:, :, :width]
    grads_out = arranged[:, :, width:]
    direct_shape = (device_count, shards_here, slot_count, width)
    rows_in, grads_in = (
        lax.all_to_all(rows_out.reshape(direct_shape), AXES, split_axis=0, concat_axis=0, tiled=True),
        lax.all_to_all(grads_out.reshape(direct_shape), AXES, split_axis=0, concat_axis=0, tiled=True),
    )
    device_index = lax.axis_index("grp") * inner_count + lax.axis_index("sp")
    first_shard = device_index * shards_here
    scales_here = lax.dynamic_slice_in_dim(code_scales, first_shard % expert_count, shards_here, 0)
    scale_gate = scales_here[:, 0][None, :, None, None]
    scale_up = scales_here[:, 1][None, :, None, None]
    scale_down = scales_here[:, 2][None, :, None, None]

    def product(spec, left, right):
        return jnp.einsum(spec, left, right, preferred_element_type=jnp.float32)

    gate_value = product("nicd,idh->nich", rows_in, gate_codes) * scale_gate
    up_value = product("nicd,idh->nich", rows_in, up_codes) * scale_up
    sigmoid_gate, silu_gate = silu_parts(gate_value)
    activation = (silu_gate * up_value).astype(jnp.bfloat16)
    expert_part = product("nich,ihd->nicd", activation, down_codes) * scale_down
    grad_activation = product("nicd,ihd->nich", grads_in, down_codes) * scale_down
    grad_gate = (
        grad_activation * up_value * sigmoid_gate * (1.0 + gate_value * (1.0 - sigmoid_gate))
    ).astype(jnp.bfloat16)
    grad_up = (grad_activation * silu_gate).astype(jnp.bfloat16)
    grad_part = product("nich,idh->nicd", grad_gate, gate_codes) * scale_gate
    grad_part = grad_part + product("nich,idh->nicd", grad_up, up_codes) * scale_up
    returned_part, returned_grad = (
        lax.all_to_all(expert_part.astype(BF16), AXES, split_axis=0, concat_axis=0, tiled=True),
        lax.all_to_all(grad_part.astype(BF16), AXES, split_axis=0, concat_axis=0, tiled=True),
    )
    returned_part = returned_part.reshape(2 * expert_count, slot_count, width).astype(F32)
    returned_grad = returned_grad.reshape(2 * expert_count, slot_count, width).astype(F32)
    expert_out = (returned_part[:expert_count] + returned_part[expert_count:]).astype(jnp.bfloat16)
    expert_grad = (returned_grad[:expert_count] + returned_grad[expert_count:]).astype(jnp.bfloat16)
    gathered = jnp.concatenate(
        [expert_out.reshape(-1, width), expert_grad.reshape(-1, width)], axis=1
    )
    picked = jnp.dot(placing, gathered, preferred_element_type=jnp.float32)
    picked_out = picked[:, :width].reshape(tok_rows, top_count, width)
    picked_grad = picked[:, width:].reshape(tok_rows, top_count, width)
    output = jnp.sum(route_weight[:, :, None] * picked_out, axis=1).astype(jnp.bfloat16)
    d_route = jnp.sum(d_output.astype(jnp.float32)[:, None, :] * picked_out, axis=2)
    d_tokens = jnp.sum(picked_grad, axis=1).astype(jnp.bfloat16)
    return (output, d_tokens, d_route)


def hub_onehots(pos_ref, info, slots, experts):
    plane, here = pos_ref[0], pos_ref[1]
    far = jnp.where(here % 2 == 0, ROW, COL)
    tokens = info.shape[1]
    rows = 4 * experts * 2 * slots
    row = lax.broadcasted_iota(jnp.int32, (rows, 1), 0)
    message = row // (2 * slots * experts)
    expert = (row // (2 * slots)) % experts
    side = (row // slots) % 2
    base = (plane % 2) * 8
    device = jnp.where(
        message == 0,
        base + here,
        jnp.where(
            message == 1,
            base + (here ^ CORE),
            jnp.where(message == 2, base + (here ^ far), base + (here ^ far ^ CORE)),
        ),
    )
    cell = ((side * 16 + device) * experts + expert) * slots + row % slots
    column = lax.broadcasted_iota(jnp.int32, (1, tokens), 1)
    partner = (column // (tokens // 2)) * 16 * experts
    first = (partner + info[0:1].astype(jnp.int32)) * slots + info[2:3].astype(jnp.int32)
    second = (partner + info[1:2].astype(jnp.int32)) * slots + info[3:4].astype(jnp.int32)
    weight_first = info[4:5] + info[6:7] + info[8:9]
    weight_second = info[5:6] + info[7:8] + info[9:10]
    return first == cell, second == cell, weight_first, weight_second


def routing(own_ref, other_ref):
    return jnp.concatenate([own_ref[...], other_ref[...]], axis=1).astype(F32)


def dot_nt(left, right):
    return lax.dot_general(left, right, (((1,), (1,)), ((), ())), preferred_element_type=F32)


def dot_tn(left, right):
    return lax.dot_general(left, right, (((0,), (0,)), ((), ())), preferred_element_type=F32)


def pack_kernel(
    slots, experts, scaled, pos_ref, own_info, other_info, own_ref, other_ref, kept_ref, core_ref, far_ref
):
    first, second, weight_first, weight_second = hub_onehots(
        pos_ref, routing(own_info, other_info), slots, experts
    )
    chosen = (first | second).astype(F32).astype(BF16)
    half = own_ref.shape[1]
    rows = dot_nt(chosen[:, :half], own_ref[...]) + dot_nt(chosen[:, half:], other_ref[...])
    if scaled:
        weight = jnp.where(first, weight_first, 0.0) + jnp.where(second, weight_second, 0.0)
        rows = rows * jnp.sum(weight, axis=1, keepdims=True)
    rows = rows.astype(BF16)
    size = rows.shape[0] // 4
    kept_ref[...] = rows[:size]
    core_ref[...] = rows[size : 2 * size]
    far_ref[0] = rows[2 * size : 3 * size]
    far_ref[1] = rows[3 * size :]


def combine_kernel(
    slots, experts, pos_ref, own_info, other_info, kept_ref, core_ref, far_ref, own_ref, other_ref
):
    first, second, _, _ = hub_onehots(pos_ref, routing(own_info, other_info), slots, experts)
    chosen = (first | second).astype(F32).astype(BF16)
    rows = jnp.concatenate([kept_ref[...], core_ref[0], far_ref[0], far_ref[1]], axis=0)
    half = own_ref.shape[1]
    sums = dot_tn(rows, chosen)
    own_ref[...] = sums[:, :half]
    other_ref[...] = sums[:, half:].astype(BF16)


def combine_out_kernel(
    slots,
    experts,
    pos_ref,
    own_info,
    other_info,
    kept_ref,
    core_ref,
    far_ref,
    d_own_ref,
    d_other_ref,
    own_ref,
    other_ref,
    route_ref,
):
    first, second, weight_first, weight_second = hub_onehots(
        pos_ref, routing(own_info, other_info), slots, experts
    )
    weight = jnp.where(first, weight_first, 0.0) + jnp.where(second, weight_second, 0.0)
    high = weight.astype(BF16)
    low = (weight - high.astype(F32)).astype(BF16)
    rows = jnp.concatenate([kept_ref[...], core_ref[0], far_ref[0], far_ref[1]], axis=0)
    half = own_ref.shape[1]
    sums = dot_tn(rows, high) + dot_tn(rows, low)
    own_ref[...] = sums[:, :half]
    other_ref[...] = sums[:, half:].astype(BF16)
    for side, d_ref in enumerate((d_own_ref, d_other_ref)):
        span = slice(side * half, (side + 1) * half)
        dots = jnp.dot(rows, d_ref[...], preferred_element_type=F32)
        for choice, mask in enumerate((first, second)):
            route_ref[side, choice : choice + 1, :] = jnp.sum(
                jnp.where(mask[:, span], dots, 0.0), axis=0, keepdims=True
            )


def rows_of(refs):
    parts = []
    for kept_ref, far_ref, core_ref in zip(refs[0::3], refs[1::3], refs[2::3]):
        parts += [kept_ref[...], far_ref[0], core_ref[0], core_ref[1]]
    return jnp.concatenate(parts, axis=0)


def put_rows(refs, value):
    size = refs[0].shape[0]
    for plane in range(len(refs) // 3):
        kept_ref, far_ref, core_ref = refs[3 * plane : 3 * plane + 3]
        part = [value[(4 * plane + n) * size : (4 * plane + n + 1) * size] for n in range(4)]
        kept_ref[...], far_ref[...], core_ref[0], core_ref[1] = part


def experts_kernel(experts, planes, pos_ref, scales_ref, *refs):
    count = 3 * planes
    x_refs, d_refs, refs = refs[:count], refs[count : 2 * count], refs[2 * count :]
    (gate_ref, up_ref, down_ref), out_refs, grad_refs = refs[:3], refs[3 : 3 + count], refs[3 + count :]
    expert = ((pos_ref[0] % 2) * 8 + pos_ref[1]) * experts + pl.program_id(0)
    scale_gate, scale_up, scale_down = [scales_ref[expert, n] for n in range(3)]
    x = rows_of(x_refs)
    gate_value = dot_nt(x, gate_ref[0]) * scale_gate
    up_value = dot_nt(x, up_ref[0]) * scale_up
    grad_activation = dot_nt(rows_of(d_refs), down_ref[0]) * scale_down
    sigmoid_gate, silu_gate = silu_parts(gate_value)
    activation = (silu_gate * up_value).astype(BF16)
    grad_gate = grad_activation * up_value * sigmoid_gate * (1.0 + gate_value * (1.0 - sigmoid_gate))
    grad_gate = grad_gate.astype(BF16)
    grad_up = (grad_activation * silu_gate).astype(BF16)
    part = jnp.dot(activation, down_ref[0], preferred_element_type=F32) * scale_down
    put_rows(out_refs, part.astype(BF16))
    part = jnp.dot(grad_gate, gate_ref[0], preferred_element_type=F32) * scale_gate
    part = part + jnp.dot(grad_up, up_ref[0], preferred_element_type=F32) * scale_up
    put_rows(grad_refs, part.astype(BF16))


SMEM_SPEC = pl.BlockSpec(memory_space=pltpu.SMEM)
PARAMS = pltpu.CompilerParams(vmem_limit_bytes=VMEM_BYTES)


def whole(*shape):
    return pl.BlockSpec(shape, lambda i: (0,) * len(shape))


def after(value, *others):
    return lax.optimization_barrier((value, *others))[0]


def with_core(value):
    return lax.ppermute(value, AXES, [(n, n ^ CORE) for n in range(32)])


def with_near(value):
    return lax.ppermute(value, AXES, [(n, n ^ (ROW if n & CORE else COL)) for n in range(32)])


def with_far(value):
    return lax.ppermute(value, AXES, [(n, n ^ (COL if n & CORE else ROW)) for n in range(32)])


def to_next_plane(value, by):
    return lax.ppermute(value, AXES, [(n, (n + 8 * by) % 32) for n in range(32)])


def per_device_planes(
    tokens, d_output, expert_ids, route_weight, gate_codes, up_codes, down_codes, code_scales
):
    tokens, d_output, ids = tokens.T, d_output.T, expert_ids.T
    gate_codes, up_codes = jnp.swapaxes(gate_codes, 1, 2), jnp.swapaxes(up_codes, 1, 2)
    width, tok_rows = tokens.shape
    experts, hidden = gate_codes.shape[:2]
    expert_count = code_scales.shape[0]
    slots = 2 * tok_rows * ids.shape[0] // expert_count
    message = experts * 2 * slots
    pos = jnp.stack([lax.axis_index("grp"), lax.axis_index("sp")]).astype(jnp.int32)

    earlier = jnp.arange(tok_rows)[:, None] < jnp.arange(tok_rows)[None, :]
    same = (ids[:, None, :, None] == ids[None, :, None, :]) & earlier
    rank = jnp.sum(same.astype(jnp.int32), axis=(0, 2))
    weight = route_weight.T
    high = lax.reduce_precision(weight, 8, 7)
    middle = lax.reduce_precision(weight - high, 8, 7)
    low = weight - high - middle
    info = [ids.astype(F32), rank.astype(F32), high, middle, low]
    info = jnp.concatenate(info + [jnp.zeros((6, tok_rows), F32)], axis=0).astype(BF16)
    tokens = jnp.concatenate([tokens, info], axis=0)
    info_rows = info.shape[0]

    one_type = jax.ShapeDtypeStruct((message, width), BF16)
    two_type = jax.ShapeDtypeStruct((2, message, width), BF16)
    info_spec = pl.BlockSpec((info_rows, tok_rows), lambda i: (width // info_rows, 0))
    block_spec = whole(width, tok_rows)
    one_spec, two_spec = whole(message, width), whole(2, message, width)
    first_spec = pl.BlockSpec((1, message, width), lambda i: (0, 0, 0))
    small_cost = pl.CostEstimate(
        flops=4 * message * 4 * tok_rows * width, bytes_accessed=12 * message * width, transcendentals=0
    )

    def spread(rows, infos, scaled):
        arrived, raw = [], []
        for step in range(4):
            other = with_near(rows)
            raw.append((rows, other))
            kept, core, far = pl.pallas_call(
                functools.partial(pack_kernel, slots, experts, scaled),
                out_shape=[one_type, one_type, two_type],
                grid=(1,),
                in_specs=[SMEM_SPEC] + [info_spec] * 2 + [block_spec] * 2,
                out_specs=[one_spec, one_spec, two_spec],
                compiler_params=PARAMS,
                cost_estimate=small_cost,
                name="pack_gradients" if scaled else "pack_tokens",
            )(pos, *(infos or raw)[step], rows, other)
            far = with_far(far)
            core = with_core(jnp.stack([core, far[1]]))
            arrived += [kept, far, core]
            if step < 3:
                rows = to_next_plane(rows, 1)
        return arrived, raw

    token_rows, infos = spread(tokens, None, False)
    grad_rows, raw_grads = spread(d_output, infos, True)

    expert_rows = 2 * slots
    kept_in = pl.BlockSpec((expert_rows, width), lambda i: (i, 0))
    far_in = pl.BlockSpec((1, expert_rows, width), lambda i: (0, i, 0))
    core_in = pl.BlockSpec((2, expert_rows, width), lambda i: (0, i, 0))
    code_spec = pl.BlockSpec((1, hidden, width), lambda i: (i, 0, 0))

    def run_experts(steps):
        planes = len(steps)
        span = slice(3 * steps[0], 3 * steps[0] + 3 * planes)
        row_count = planes * 4 * expert_rows
        done = pl.pallas_call(
            functools.partial(experts_kernel, experts, planes),
            out_shape=[one_type, one_type, two_type] * (2 * planes),
            grid=(experts,),
            in_specs=[SMEM_SPEC] * 2
            + [kept_in, far_in, core_in] * (2 * planes)
            + [code_spec] * 3,
            out_specs=[kept_in, kept_in, core_in] * (2 * planes),
            compiler_params=PARAMS,
            cost_estimate=pl.CostEstimate(
                flops=experts * row_count * width * hidden * 12,
                bytes_accessed=experts * width * hidden * 6,
                transcendentals=experts * row_count * hidden,
            ),
            name="experts",
        )(pos, code_scales, *token_rows[span], *grad_rows[span], gate_codes, up_codes, down_codes)
        return done[: 3 * planes], done[3 * planes :]

    parts, grads = run_experts((0, 1, 2, 3))

    own_type = jax.ShapeDtypeStruct((width, tok_rows), F32)
    other_type = jax.ShapeDtypeStruct((width, tok_rows), BF16)
    route_type = jax.ShapeDtypeStruct((2, 2, tok_rows), F32)

    def gather(rows, outputs):
        total, routes, last = None, [None] * 4, []
        for step in (3, 2, 1, 0):
            kept, far, core = rows[3 * step : 3 * step + 3]
            core = with_core(core)
            far = with_far(after(jnp.stack([far, core[1]]), *last))
            own, other, *route = pl.pallas_call(
                functools.partial(combine_out_kernel if outputs else combine_kernel, slots, experts),
                out_shape=[own_type, other_type] + [route_type] * outputs,
                grid=(1,),
                in_specs=[SMEM_SPEC]
                + [info_spec] * 2
                + [one_spec, first_spec, two_spec]
                + [block_spec] * (2 * outputs),
                out_specs=[block_spec] * 2 + [whole(2, 2, tok_rows)] * outputs,
                compiler_params=PARAMS,
                cost_estimate=small_cost,
                name="sum_outputs" if outputs else "sum_gradients",
            )(pos, *infos[step], kept, core, far, *(raw_grads[step] if outputs else ()))
            routes[step] = route
            other = with_near(other)
            last = [other]
            value = own + other.astype(F32)
            if total is not None:
                value = value + to_next_plane(total, -1).astype(F32)
            total = value.astype(BF16)
        return total, routes

    output, routes = gather(parts, 1)
    route = jnp.stack([r[0][0] for r in routes]) + with_near(jnp.stack([r[0][1] for r in routes]))
    d_route = route[0]
    for step in (1, 2, 3):
        d_route = d_route + to_next_plane(route[step], -step)
    d_tokens, _ = gather(grads, 0)
    return (output.T, d_tokens.T, d_route.T)


def solution(mesh):
    planes = mesh.shape["grp"] == 4 and mesh.shape["sp"] == 8
    spec = P(AXES, None)
    codes = P(AXES, None, None)
    return jax.shard_map(
        per_device_planes if planes else per_device,
        mesh=mesh,
        in_specs=(spec, spec, spec, spec, codes, codes, codes, P()),
        out_specs=(spec, spec, spec),
        check_vma=False,
    )
```

time: 969 us -> 362 us (0.37)
  waiting for transfers between devices: 625 us -> 146 us
  blocking collectives: 140 us -> 0 us
  Pallas kernels: 0 us -> 101 us
  matrix products: 86.2 us -> 0 us
  starting transfers between devices: 11.7 us -> 70.5 us
  local copies, waits for them, and re-layouts: 53.4 us -> 23.6 us
  other arithmetic: 41.1 us -> 19 us
    all_to_all x3 -> x0, waiting for transfers between devices: 625 us -> none  [the longest x1 260 us: per_device(): lax.all_to_all(expert_part, ('grp', 'sp'), split_axis=0, concat_axis=0, t...]
    ppermute x0 -> x64, waiting for transfers between devices: none -> 146 us  [the longest x15 63.1 us: to_next_plane(): lax.ppermute(value, AXES, [(n, (n + 8 * by) % 32) for n in range(32)])]
    all_to_all x1 -> x0, blocking collectives: 140 us -> none  [per_device(): lax.all_to_all(grads_out.reshape(direct_shape), ('grp', 'sp'), split_axis...]
    pallas_call x0 -> x17, Pallas kernels: none -> 101 us  [the longest x1 38.9 us: run_experts(): pl.pallas_call(functools.partial(experts_kernel, experts, planes), out_sh...]
    dot_general x8 -> x0, matrix products: 86.2 us -> none  [the longest x1 18.2 us: per_device(): jnp.einsum('nich,idh->nicd', grad_gate, gate_codes, preferred_element_typ...]
    ppermute x0 -> x64, starting transfers between devices: none -> 70.5 us  [the longest x15 27.2 us: to_next_plane(): lax.ppermute(value, AXES, [(n, (n + 8 * by) % 32) for n in range(32)])]
    concatenate x1 -> x0, other arithmetic: 14.5 us -> none  [per_device(): arranged = jnp.concatenate([arranged, arranged], axis=0)]
    reduce_sum x4 -> x1, other arithmetic: 13.8 us -> 0.87 us  [per_device_planes(): rank = jnp.sum(same.astype(jnp.int32), axis=(0, 2))]
  transfers between devices with their start and end apart: 3 -> 64, of which waited for: 3 -> 29; matrix products, arithmetic and copies ran while one was open for 5% -> 6% of each run, Pallas kernels for 0% -> 17%
where the time goes in v1:
time: 362 us; the launch traced here: 361 us
  waiting for transfers between devices  146 us (40%)
  Pallas kernels  101 us (28%)
  starting transfers between devices  70.5 us (19%)
  local copies, waits for them, and re-layouts  23.6 us (7%)
  other arithmetic  19 us (5%)
    ppermute x15, waiting for transfers between devices, to_next_plane(): lax.ppermute(value, AXES, [(n, (n + 8 * by) % 32) for n in range(32)])  63.1 us
    ppermute x17, waiting for transfers between devices, with_near(): lax.ppermute(value, AXES, [(n, n ^ (ROW if n & CORE else COL)) for n in r...  40.4 us
    pallas_call x1, Pallas kernels, run_experts(): pl.pallas_call(functools.partial(experts_kernel, experts, planes), out_sh...  38.9 us
    ppermute x16, waiting for transfers between devices, with_far(): lax.ppermute(value, AXES, [(n, n ^ (COL if n & CORE else ROW)) for n in r...  38.5 us
    pallas_call x8, Pallas kernels, gather(): pl.pallas_call(functools.partial(combine_out_kernel if outputs else combi...  34.2 us
    pallas_call x8, Pallas kernels, spread(): pl.pallas_call(functools.partial(pack_kernel, slots, experts, scaled), ou...  27.6 us
    ppermute x15, starting transfers between devices, to_next_plane(): lax.ppermute(value, AXES, [(n, (n + 8 * by) % 32) for n in range(32)])  27.2 us
    ppermute x17, starting transfers between devices, with_near(): lax.ppermute(value, AXES, [(n, n ^ (ROW if n & CORE else COL)) for n in r...  21.3 us
  transfers between devices with their start and end apart: 64, of which 29 were waited for; matrix products, arithmetic and copies ran while one was open for 6% of the time, Pallas kernels for 17%

profile of v1, /device:TPU:0, one launch (start us, length us, event | category | flops | bytes accessed | tf_op | source)
XLA Modules:
  0.0 361.3 jit_solution(15484125384816819918)
XLA Ops:
  0.6 3.1 collective-permute-start.18
  6.0 2.9 concatenate.6.own_info.own_ref
  12.6 10.8 %collective-permute-done.18.own_ref.d_own_ref = bf16[2880,128]{1,0:T(8,128)(2,1)} collective-permute-done((bf16[2880,128]{1,0:T(8,128)(2,1)}, bf16[2880,128]{1,0:T(8,128)(2,1)}, u32[]{:S(2)}, u32[]{:S(2)}) %collective-permute-start.18) | collective-permute-done | bytes 737312 | tf_op jit(solution)/shard_map/ppermute | solution.py:267
  25.1 14.1 %collective-permute-done.3.own_info.own_ref = bf16[2896,128]{1,0:T(8,128)(2,1)S(1)} collective-permute-done((bf16[2896,128]{1,0:T(8,128)(2,1)S(1)}, bf16[2896,128]{1,0:T(8,128)(2,1)S(1)}, u32[]{:S(2)}, u32[]{:S(2)}) %collective-permute-start.3) | collective-permute-done | bytes 741408 | tf_op jit(solution)/shard_map/ppermute | solution.py:267
  43.4 3.5 pack_gradients.4
  48.4 3.4 pack_tokens.4
  51.8 3.3 collective-permute-done.22.own_ref.d_own_ref
  55.1 1.8 collective-permute-start.1
  56.8 14.1 %collective-permute-done.7.own_info.own_ref = bf16[2896,128]{1,0:T(8,128)(2,1)} collective-permute-done((bf16[2896,128]{1,0:T(8,128)(2,1)S(1)}, bf16[2896,128]{1,0:T(8,128)(2,1)}, u32[]{:S(2)}, u32[]{:S(2)}) %collective-permute-start.7) | collective-permute-done | bytes 741408 | tf_op jit(solution)/shard_map/ppermute | solution.py:267
  71.9 3.4 pack_gradients.5
  78.6 3.5 pack_tokens.5
  83.5 3.2 collective-permute-done.26.own_ref.d_own_ref
  89.5 5.8 %collective-permute-done.20.refs_16_ = bf16[2,64,2880]{2,1,0:T(8,128)(2,1)S(1)} collective-permute-done((bf16[2,64,2880]{2,1,0:T(8,128)(2,1)}, bf16[2,64,2880]{2,1,0:T(8,128)(2,1)S(1)}, u32[]{:S(2)}, u32[]{:S(2)}) %collective-permute-start.20) | collective-permute-done | bytes 737312 | tf_op jit(solution)/shard_map/ppermute | solution.py:263
  97.0 4.7 %collective-permute-done.11.own_info.own_ref = bf16[2896,128]{1,0:T(8,128)(2,1)S(1)} collective-permute-done((bf16[2896,128]{1,0:T(8,128)(2,1)}, bf16[2896,128]{1,0:T(8,128)(2,1)S(1)}, u32[]{:S(2)}, u32[]{:S(2)}) %collective-permute-start.11) | collective-permute-done | bytes 741408 | tf_op jit(solution)/shard_map/ppermute | solution.py:267
  104.2 7.3 %collective-permute-done.5.refs_4_ = bf16[2,64,2880]{2,1,0:T(8,128)(2,1)S(1)} collective-permute-done((bf16[2,64,2880]{2,1,0:T(8,128)(2,1)}, bf16[2,64,2880]{2,1,0:T(8,128)(2,1)S(1)}, u32[]{:S(2)}, u32[]{:S(2)}) %collective-permute-start.5) | collective-permute-done | bytes 737312 | tf_op jit(solution)/shard_map/ppermute | solution.py:263
  113.4 3.5 pack_gradients.6
  116.8 1.8 collective-permute-start.24
  118.6 3.4 pack_tokens.6
  122.5 6.2 %collective-permute-done.12.other_info.other_ref = bf16[2896,128]{1,0:T(8,128)(2,1)S(1)} collective-permute-done((bf16[2896,128]{1,0:T(8,128)(2,1)S(1)}, bf16[2896,128]{1,0:T(8,128)(2,1)S(1)}, u32[]{:S(2)}, u32[]{:S(2)}) %collective-permute-start.12) | collective-permute-done | bytes 741408 | tf_op jit(solution)/shard_map/ppermute | solution.py:259
  129.5 3.5 pack_gradients.7
  133.8 3.5 pack_tokens.7
  139.7 1.8 collective-permute-done.9.refs_7_
  142.7 7.0 %collective-permute-done.28.refs_22_ = bf16[2,64,2880]{2,1,0:T(8,128)(2,1)S(1)} collective-permute-done((bf16[2,64,2880]{2,1,0:T(8,128)(2,1)}, bf16[2,64,2880]{2,1,0:T(8,128)(2,1)S(1)}, u32[]{:S(2)}, u32[]{:S(2)}) %collective-permute-start.28) | collective-permute-done | bytes 737312 | tf_op jit(solution)/shard_map/ppermute | solution.py:263
  149.7 8.0 %collective-permute-done.13.refs_10_ = bf16[2,64,2880]{2,1,0:T(8,128)(2,1)S(1)} collective-permute-done((bf16[2,64,2880]{2,1,0:T(8,128)(2,1)}, bf16[2,64,2880]{2,1,0:T(8,128)(2,1)S(1)}, u32[]{:S(2)}, u32[]{:S(2)}) %collective-permute-start.13) | collective-permute-done | bytes 737312 | tf_op jit(solution)/shard_map/ppermute | solution.py:263
  163.6 38.9 %experts.1 = (bf16[64,2880]{1,0:T(8,128)(2,1)}, bf16[64,2880]{1,0:T(8,128)(2,1)}, bf16[2,64,2880]{2,1,0:T(8,128)(2,1)}, bf16[64,2880]{1,0:T(8,128)(2,1)}, bf16[6...) custom-call(s32[2]{0:T(128)} %pad_add_fusion.pos_ref, ...), custom_call_target="tpu_custom_call" | custom-call | flops 25480396800 | bytes 49766400 | tf_op jit(solution)/shard_map/experts/pallas_call | solution.py:339
  212.8 7.1 %collective-permute-done.34.far_ref = bf16[2,64,2880]{2,1,0:T(8,128)(2,1)S(1)} collective-permute-done((bf16[2,64,2880]{2,1,0:T(8,128)(2,1)S(1)}, bf16[2,64,2880]{2,1,0:T(8,128)(2,1)S(1)}, u32[]{:S(2)}, u32[]{:S(2)}) %collective-permute-start.34) | collective-permute-done | bytes 737312 | tf_op jit(solution)/shard_map/ppermute | solution.py:263
  220.9 5.1 %sum_outputs.4 = (f32[2880,128]{1,0:T(8,128)}, bf16[2880,128]{1,0:T(8,128)(2,1)}, f32[2,2,128]{2,1,0:T(2,128)}) custom-call(s32[2]{0:T(128)} %pad_add_fusion.pos_ref, bf16[2896,128]{1,0:T(8,128)(2,1)} %copy-done.5, bf16[2896,128]{1,0:T(8,128)(2,1)} %copy-done.6, bf16[64,2880]{1,0:T(8,128)(2,1)} %get-tuple-element.110.kept_ref, ...), custom_call_target="tpu_custom_call" | custom-call | flops 377487360 | bytes 2211840 | tf_op jit(solution)/shard_map/sum_outputs/pallas_call | solution.py:369
  228.8 3.5 sum_gradients.4
  233.1 4.6 %collective-permute-done.35 = bf16[2880,128]{1,0:T(8,128)(2,1)} collective-permute-done((bf16[2880,128]{1,0:T(8,128)(2,1)}, bf16[2880,128]{1,0:T(8,128)(2,1)}, u32[]{:S(2)}, u32[]{:S(2)}) %collective-permute-start.35) | collective-permute-done | bytes 737312 | tf_op jit(solution)/shard_map/ppermute | solution.py:259
  239.2 2.1 add_convert_fusion.7
  241.4 3.5 collective-permute-start.42
  244.9 7.1 %collective-permute-done.50 = bf16[2880,128]{1,0:T(8,128)(2,1)S(1)} collective-permute-done((bf16[2880,128]{1,0:T(8,128)(2,1)}, bf16[2880,128]{1,0:T(8,128)(2,1)S(1)}, u32[]{:S(2)}, u32[]{:S(2)}) %collective-permute-start.50) | collective-permute-done | bytes 737312 | tf_op jit(solution)/shard_map/ppermute | solution.py:259
  254.4 5.1 %sum_outputs.5 = (f32[2880,128]{1,0:T(8,128)}, bf16[2880,128]{1,0:T(8,128)(2,1)}, f32[2,2,128]{2,1,0:T(2,128)}) custom-call(s32[2]{0:T(128)} %pad_add_fusion.pos_ref, bf16[2896,128]{1,0:T(8,128)(2,1)} %collective-permute-done.7.own_info.own_ref, bf16[2896,128]{1,0:T(8,128)(2,1)} %copy-done.4, bf16[64,2880]{1,0:T(8,128)(2,1)} %get-tuple-element.107.kept_ref, ...), custom_call_target="tpu_custom_call" | custom-call | flops 377487360 | bytes 2211840 | tf_op jit(solution)/shard_map/sum_outputs/pallas_call | solution.py:369
  261.1 3.5 collective-permute-start.57
  265.6 3.4 sum_gradients.5
  273.7 3.6 collective-permute-start.43
  277.3 9.7 %collective-permute-done.52 = bf16[2880,128]{1,0:T(8,128)(2,1)S(1)} collective-permute-done((bf16[2880,128]{1,0:T(8,128)(2,1)}, bf16[2880,128]{1,0:T(8,128)(2,1)S(1)}, u32[]{:S(2)}, u32[]{:S(2)}) %collective-permute-start.52) | collective-permute-done | bytes 737312 | tf_op jit(solution)/shard_map/ppermute | solution.py:259
  289.4 5.1 %sum_outputs.6 = (f32[2880,128]{1,0:T(8,128)}, bf16[2880,128]{1,0:T(8,128)(2,1)}, f32[2,2,128]{2,1,0:T(2,128)}) custom-call(s32[2]{0:T(128)} %pad_add_fusion.pos_ref, bf16[2896,128]{1,0:T(8,128)(2,1)} %copy-done.2, bf16[2896,128]{1,0:T(8,128)(2,1)} %copy-done.3, bf16[64,2880]{1,0:T(8,128)(2,1)} %get-tuple-element.104.kept_ref, ...), custom_call_target="tpu_custom_call" | custom-call | flops 377487360 | bytes 2211840 | tf_op jit(solution)/shard_map/sum_outputs/pallas_call | solution.py:369
  297.9 2.7 collective-permute-start.58
  301.5 3.5 sum_gradients.6
  305.0 2.1 collective-permute-start.54
  308.9 3.0 collective-permute-start.44
  311.9 11.8 %collective-permute-done.54 = bf16[2880,128]{1,0:T(8,128)(2,1)} collective-permute-done((bf16[2880,128]{1,0:T(8,128)(2,1)}, bf16[2880,128]{1,0:T(8,128)(2,1)}, u32[]{:S(2)}, u32[]{:S(2)}) %collective-permute-start.54) | collective-permute-done | bytes 737312 | tf_op jit(solution)/shard_map/ppermute | solution.py:259
  325.6 5.1 %sum_outputs.7 = (f32[2880,128]{1,0:T(8,128)}, bf16[2880,128]{1,0:T(8,128)(2,1)}, f32[2,2,128]{2,1,0:T(2,128)}) custom-call(s32[2]{0:T(128)} %pad_add_fusion.pos_ref, bf16[2896,128]{1,0:T(8,128)(2,1)} %copy-done, bf16[2896,128]{1,0:T(8,128)(2,1)} %copy-done.1, bf16[64,2880]{1,0:T(8,128)(2,1)} %get-tuple-element.101.kept_ref, ...), custom_call_target="tpu_custom_call" | custom-call | flops 377487360 | bytes 2211840 | tf_op jit(solution)/shard_map/sum_outputs/pallas_call | solution.py:369
  335.0 1.8 collective-permute-start.61
  337.9 3.4 sum_gradients.7
  341.4 3.6 collective-permute-start.59
  347.2 12.9 %collective-permute-done.59 = bf16[2880,128]{1,0:T(8,128)(2,1)S(1)} collective-permute-done((bf16[2880,128]{1,0:T(8,128)(2,1)S(1)}, bf16[2880,128]{1,0:T(8,128)(2,1)S(1)}, u32[]{:S(2)}, u32[]{:S(2)}) %collective-permute-start.59) | collective-permute-done | bytes 737312 | tf_op jit(solution)/shard_map/ppermute | solution.py:267
  (297 shorter events, 84.3 us)
Async XLA Ops:
  0.6 22.7 %collective-permute-start.18 = (bf16[2880,128]{1,0:T(8,128)(2,1)}, bf16[2880,128]{1,0:T(8,128)(2,1)}, u32[]{:S(2)}, u32[]{:S(2)}) collective-permute-start(bf16[2880,128]{1,0:T(8,128)(2,1)} %bitcast.53), channel_id=1, source_target_pairs={{0,8},{1,9},{2,10},{3,11},{4,12},{5,13},{6,14},{7,15},{8,16},{9,17... | collective-permute-start | bytes 2211848 | tf_op jit(solution)/shard_map/ppermute | solution.py:267
  8.9 30.2 %collective-permute-start.3 = (bf16[2896,128]{1,0:T(8,128)(2,1)S(1)}, bf16[2896,128]{1,0:T(8,128)(2,1)S(1)}, u32[]{:S(2)}, u32[]{:S(2)}) collective-permute-start(bf16[2896,128]{1,0:T(8,128)(2,1)S(1)} %concatenate.6.own_info.own_ref), channel_id=1, source_target_pairs={{0,8},{1,9},{2,10},{3,11},{4,12},{5,13},{6,14},{7,15},{8,16},{9,17... | collective-permute-start | bytes 2224136 | tf_op jit(solution)/shard_map/ppermute | solution.py:267
  10.5 28.7 %collective-permute-start.15 = (bf16[2880,128]{1,0:T(8,128)(2,1)S(1)}, bf16[2880,128]{1,0:T(8,128)(2,1)S(1)}, u32[]{:S(2)}, u32[]{:S(2)}) collective-permute-start(bf16[2880,128]{1,0:T(8,128)(2,1)S(1)} %bitcast.56), channel_id=1, source_target_pairs={{0,2},{1,5},{2,0},{3,7},{4,6},{5,1},{6,4},{7,3},{8,10},{9,13},{10,... | collective-permute-start | bytes 2211848 | tf_op jit(solution)/shard_map/ppermute | solution.py:259
  12.0 30.5 %collective-permute-start = (bf16[2896,128]{1,0:T(8,128)(2,1)S(1)}, bf16[2896,128]{1,0:T(8,128)(2,1)S(1)}, u32[]{:S(2)}, u32[]{:S(2)}) collective-permute-start(bf16[2896,128]{1,0:T(8,128)(2,1)S(1)} %concatenate.6.own_info.own_ref), channel_id=1, source_target_pairs={{0,2},{1,5},{2,0},{3,7},{4,6},{5,1},{6,4},{7,3},{8,10},{9,13},{10,... | collective-permute-start | bytes 2224136 | tf_op jit(solution)/shard_map/ppermute | solution.py:259
  23.4 31.7 %collective-permute-start.22 = (bf16[2880,128]{1,0:T(8,128)(2,1)}, bf16[2880,128]{1,0:T(8,128)(2,1)}, u32[]{:S(2)}, u32[]{:S(2)}) collective-permute-start(bf16[2880,128]{1,0:T(8,128)(2,1)} %collective-permute-done.18.own_ref.d_own_ref), channel_id=1, source_target_pairs={{0,8},{1,9},{2,10},{3,11},{4,12},{5,13},{6,14},{7,15},{8,16},{9,17... | collective-permute-start | bytes 2211848 | tf_op jit(solution)/shard_map/ppermute | solution.py:267
  23.4 33.4 %collective-permute-start.19 = (bf16[2880,128]{1,0:T(8,128)(2,1)}, bf16[2880,128]{1,0:T(8,128)(2,1)}, u32[]{:S(2)}, u32[]{:S(2)}) collective-permute-start(bf16[2880,128]{1,0:T(8,128)(2,1)} %collective-permute-done.18.own_ref.d_own_ref), channel_id=1, source_target_pairs={{0,2},{1,5},{2,0},{3,7},{4,6},{5,1},{6,4},{7,3},{8,10},{9,13},{10,... | collective-permute-start | bytes 2211848 | tf_op jit(solution)/shard_map/ppermute | solution.py:259
  39.2 31.8 %collective-permute-start.7 = (bf16[2896,128]{1,0:T(8,128)(2,1)S(1)}, bf16[2896,128]{1,0:T(8,128)(2,1)}, u32[]{:S(2)}, u32[]{:S(2)}) collective-permute-start(bf16[2896,128]{1,0:T(8,128)(2,1)S(1)} %collective-permute-done.3.own_info.own_ref), channel_id=1, source_target_pairs={{0,8},{1,9},{2,10},{3,11},{4,12},{5,13},{6,14},{7,15},{8,16},{9,17... | collective-permute-start | bytes 2224136 | tf_op jit(solution)/shard_map/ppermute | solution.py:267
  40.1 30.9 %collective-permute-start.4 = (bf16[2896,128]{1,0:T(8,128)(2,1)S(1)}, bf16[2896,128]{1,0:T(8,128)(2,1)S(1)}, u32[]{:S(2)}, u32[]{:S(2)}) collective-permute-start(bf16[2896,128]{1,0:T(8,128)(2,1)S(1)} %collective-permute-done.3.own_info.own_ref), channel_id=1, source_target_pairs={{0,2},{1,5},{2,0},{3,7},{4,6},{5,1},{6,4},{7,3},{8,10},{9,13},{10,... | collective-permute-start | bytes 2224136 | tf_op jit(solution)/shard_map/ppermute | solution.py:259
  46.8 30.2 %collective-permute-start.16 = (bf16[2,64,2880]{2,1,0:T(8,128)(2,1)}, bf16[2,64,2880]{2,1,0:T(8,128)(2,1)S(1)}, u32[]{:S(2)}, u32[]{:S(2)}) collective-permute-start(bf16[2,64,2880]{2,1,0:T(8,128)(2,1)} %get-tuple-element.90), channel_id=1, source_target_pairs={{0,4},{1,3},{2,6},{3,1},{4,0},{5,7},{6,2},{7,5},{8,12},{9,11},{10,... | collective-permute-start | bytes 2211848 | tf_op jit(solution)/shard_map/ppermute | solution.py:263
  55.1 27.0 %collective-permute-start.1 = (bf16[2,64,2880]{2,1,0:T(8,128)(2,1)}, bf16[2,64,2880]{2,1,0:T(8,128)(2,1)S(1)}, u32[]{:S(2)}, u32[]{:S(2)}) collective-permute-start(bf16[2,64,2880]{2,1,0:T(8,128)(2,1)} %get-tuple-element.78), channel_id=1, source_target_pairs={{0,4},{1,3},{2,6},{3,1},{4,0},{5,7},{6,2},{7,5},{8,12},{9,11},{10,... | collective-permute-start | bytes 2211848 | tf_op jit(solution)/shard_map/ppermute | solution.py:263
  56.8 29.8 %collective-permute-start.26 = (bf16[2880,128]{1,0:T(8,128)(2,1)}, bf16[2880,128]{1,0:T(8,128)(2,1)S(1)}, u32[]{:S(2)}, u32[]{:S(2)}) collective-permute-start(bf16[2880,128]{1,0:T(8,128)(2,1)} %collective-permute-done.22.own_ref.d_own_ref), channel_id=1, source_target_pairs={{0,8},{1,9},{2,10},{3,11},{4,12},{5,13},{6,14},{7,15},{8,16},{9,17... | collective-permute-start | bytes 2211848 | tf_op jit(solution)/shard_map/ppermute | solution.py:267
  71.0 30.8 %collective-permute-start.11 = (bf16[2896,128]{1,0:T(8,128)(2,1)}, bf16[2896,128]{1,0:T(8,128)(2,1)S(1)}, u32[]{:S(2)}, u32[]{:S(2)}) collective-permute-start(bf16[2896,128]{1,0:T(8,128)(2,1)} %collective-permute-done.7.own_info.own_ref), channel_id=1, source_target_pairs={{0,8},{1,9},{2,10},{3,11},{4,12},{5,13},{6,14},{7,15},{8,16},{9,17... | collective-permute-start | bytes 2224136 | tf_op jit(solution)/shard_map/ppermute | solution.py:267
  75.3 20.0 %collective-permute-start.20 = (bf16[2,64,2880]{2,1,0:T(8,128)(2,1)}, bf16[2,64,2880]{2,1,0:T(8,128)(2,1)S(1)}, u32[]{:S(2)}, u32[]{:S(2)}) collective-permute-start(bf16[2,64,2880]{2,1,0:T(8,128)(2,1)} %get-tuple-element.93), channel_id=1, source_target_pairs={{0,4},{1,3},{2,6},{3,1},{4,0},{5,7},{6,2},{7,5},{8,12},{9,11},{10,... | collective-permute-start | bytes 2211848 | tf_op jit(solution)/shard_map/ppermute | solution.py:263
  77.1 34.4 %collective-permute-start.8 = (bf16[2896,128]{1,0:T(8,128)(2,1)}, bf16[2896,128]{1,0:T(8,128)(2,1)S(1)}, u32[]{:S(2)}, u32[]{:S(2)}) collective-permute-start(bf16[2896,128]{1,0:T(8,128)(2,1)} %collective-permute-done.7.own_info.own_ref), channel_id=1, source_target_pairs={{0,2},{1,5},{2,0},{3,7},{4,6},{5,1},{6,4},{7,3},{8,10},{9,13},{10,... | collective-permute-start | bytes 2224136 | tf_op jit(solution)/shard_map/ppermute | solution.py:259
  83.0 28.5 %collective-permute-start.5 = (bf16[2,64,2880]{2,1,0:T(8,128)(2,1)}, bf16[2,64,2880]{2,1,0:T(8,128)(2,1)S(1)}, u32[]{:S(2)}, u32[]{:S(2)}) collective-permute-start(bf16[2,64,2880]{2,1,0:T(8,128)(2,1)} %get-tuple-element.81), channel_id=1, source_target_pairs={{0,4},{1,3},{2,6},{3,1},{4,0},{5,7},{6,2},{7,5},{8,12},{9,11},{10,... | collective-permute-start | bytes 2211848 | tf_op jit(solution)/shard_map/ppermute | solution.py:263
  86.7 24.9 %collective-permute-start.23 = (bf16[2880,128]{1,0:T(8,128)(2,1)}, bf16[2880,128]{1,0:T(8,128)(2,1)S(1)}, u32[]{:S(2)}, u32[]{:S(2)}) collective-permute-start(bf16[2880,128]{1,0:T(8,128)(2,1)} %collective-permute-done.22.own_ref.d_own_ref), channel_id=1, source_target_pairs={{0,2},{1,5},{2,0},{3,7},{4,6},{5,1},{6,4},{7,3},{8,10},{9,13},{10,... | collective-permute-start | bytes 2211848 | tf_op jit(solution)/shard_map/ppermute | solution.py:259
  95.3 27.1 %collective-permute-start.27 = (bf16[2880,128]{1,0:T(8,128)(2,1)S(1)}, bf16[2880,128]{1,0:T(8,128)(2,1)S(1)}, u32[]{:S(2)}, u32[]{:S(2)}) collective-permute-start(bf16[2880,128]{1,0:T(8,128)(2,1)S(1)} %collective-permute-done.26.own_ref.d_own_ref), channel_id=1, source_target_pairs={{0,2},{1,5},{2,0},{3,7},{4,6},{5,1},{6,4},{7,3},{8,10},{9,13},{10,... | collective-permute-start | bytes 2211848 | tf_op jit(solution)/shard_map/ppermute | solution.py:259
  101.7 26.9 %collective-permute-start.12 = (bf16[2896,128]{1,0:T(8,128)(2,1)S(1)}, bf16[2896,128]{1,0:T(8,128)(2,1)S(1)}, u32[]{:S(2)}, u32[]{:S(2)}) collective-permute-start(bf16[2896,128]{1,0:T(8,128)(2,1)S(1)} %collective-permute-done.11.own_info.own_ref), channel_id=1, source_target_pairs={{0,2},{1,5},{2,0},{3,7},{4,6},{5,1},{6,4},{7,3},{8,10},{9,13},{10,... | collective-permute-start | bytes 2224136 | tf_op jit(solution)/shard_map/ppermute | solution.py:259
  111.5 47.5 %collective-permute-start.17 = (bf16[2,64,2880]{2,1,0:T(8,128)(2,1)S(1)}, bf16[2,64,2880]{2,1,0:T(8,128)(2,1)}, u32[]{:S(2)}, u32[]{:S(2)}) collective-permute-start(bf16[2,64,2880]{2,1,0:T(8,128)(2,1)S(1)} %pad_maximum_fusion.4), channel_id=1, source_target_pairs={{0,1},{1,0},{2,3},{3,2},{4,5},{5,4},{6,7},{7,6},{8,9},{9,8},{10,11... | collective-permute-start | bytes 2211848 | tf_op jit(solution)/shard_map/ppermute | solution.py:255
  116.8 21.8 %collective-permute-start.24 = (bf16[2,64,2880]{2,1,0:T(8,128)(2,1)}, bf16[2,64,2880]{2,1,0:T(8,128)(2,1)S(1)}, u32[]{:S(2)}, u32[]{:S(2)}) collective-permute-start(bf16[2,64,2880]{2,1,0:T(8,128)(2,1)} %get-tuple-element.96), channel_id=1, source_target_pairs={{0,4},{1,3},{2,6},{3,1},{4,0},{5,7},{6,2},{7,5},{8,12},{9,11},{10,... | collective-permute-start | bytes 2211848 | tf_op jit(solution)/shard_map/ppermute | solution.py:263
  122.1 19.5 %collective-permute-start.9 = (bf16[2,64,2880]{2,1,0:T(8,128)(2,1)}, bf16[2,64,2880]{2,1,0:T(8,128)(2,1)S(1)}, u32[]{:S(2)}, u32[]{:S(2)}) collective-permute-start(bf16[2,64,2880]{2,1,0:T(8,128)(2,1)} %get-tuple-element.84), channel_id=1, source_target_pairs={{0,4},{1,3},{2,6},{3,1},{4,0},{5,7},{6,2},{7,5},{8,12},{9,11},{10,... | collective-permute-start | bytes 2211848 | tf_op jit(solution)/shard_map/ppermute | solution.py:263
  133.0 16.6 %collective-permute-start.28 = (bf16[2,64,2880]{2,1,0:T(8,128)(2,1)}, bf16[2,64,2880]{2,1,0:T(8,128)(2,1)S(1)}, u32[]{:S(2)}, u32[]{:S(2)}) collective-permute-start(bf16[2,64,2880]{2,1,0:T(8,128)(2,1)} %get-tuple-element.99), channel_id=1, source_target_pairs={{0,4},{1,3},{2,6},{3,1},{4,0},{5,7},{6,2},{7,5},{8,12},{9,11},{10,... | collective-permute-start | bytes 2211848 | tf_op jit(solution)/shard_map/ppermute | solution.py:263
  137.3 20.4 %collective-permute-start.13 = (bf16[2,64,2880]{2,1,0:T(8,128)(2,1)}, bf16[2,64,2880]{2,1,0:T(8,128)(2,1)S(1)}, u32[]{:S(2)}, u32[]{:S(2)}) collective-permute-start(bf16[2,64,2880]{2,1,0:T(8,128)(2,1)} %get-tuple-element.87), channel_id=1, source_target_pairs={{0,4},{1,3},{2,6},{3,1},{4,0},{5,7},{6,2},{7,5},{8,12},{9,11},{10,... | collective-permute-start | bytes 2211848 | tf_op jit(solution)/shard_map/ppermute | solution.py:263
  138.7 20.8 %collective-permute-start.2 = (bf16[2,64,2880]{2,1,0:T(8,128)(2,1)S(1)}, bf16[2,64,2880]{2,1,0:T(8,128)(2,1)S(1)}, u32[]{:S(2)}, u32[]{:S(2)}) collective-permute-start(bf16[2,64,2880]{2,1,0:T(8,128)(2,1)S(1)} %copy-done.30), channel_id=1, source_target_pairs={{0,1},{1,0},{2,3},{3,2},{4,5},{5,4},{6,7},{7,6},{8,9},{9,8},{10,11... | collective-permute-start | bytes 2211848 | tf_op jit(solution)/shard_map/ppermute | solution.py:255
  141.6 18.0 %collective-permute-start.21 = (bf16[2,64,2880]{2,1,0:T(8,128)(2,1)S(1)}, bf16[2,64,2880]{2,1,0:T(8,128)(2,1)S(1)}, u32[]{:S(2)}, u32[]{:S(2)}) collective-permute-start(bf16[2,64,2880]{2,1,0:T(8,128)(2,1)S(1)} %pad_maximum_fusion.5), channel_id=1, source_target_pairs={{0,1},{1,0},{2,3},{3,2},{4,5},{5,4},{6,7},{7,6},{8,9},{9,8},{10,11... | collective-permute-start | bytes 2211848 | tf_op jit(solution)/shard_map/ppermute | solution.py:255
  149.6 12.4 %collective-permute-start.6 = (bf16[2,64,2880]{2,1,0:T(8,128)(2,1)S(1)}, bf16[2,64,2880]{2,1,0:T(8,128)(2,1)}, u32[]{:S(2)}, u32[]{:S(2)}) collective-permute-start(bf16[2,64,2880]{2,1,0:T(8,128)(2,1)S(1)} %pad_maximum_fusion.1), channel_id=1, source_target_pairs={{0,1},{1,0},{2,3},{3,2},{4,5},{5,4},{6,7},{7,6},{8,9},{9,8},{10,11... | collective-permute-start | bytes 2211848 | tf_op jit(solution)/shard_map/ppermute | solution.py:255
  207.2 19.6 %collective-permute-start.47 = (bf16[2,64,2880]{2,1,0:T(8,128)(2,1)}, bf16[2,64,2880]{2,1,0:T(8,128)(2,1)S(1)}, u32[]{:S(2)}, u32[]{:S(2)}) collective-permute-start(bf16[2,64,2880]{2,1,0:T(8,128)(2,1)} %get-tuple-element.131), channel_id=1, source_target_pairs={{0,1},{1,0},{2,3},{3,2},{4,5},{5,4},{6,7},{7,6},{8,9},{9,8},{10,11... | collective-permute-start | bytes 2211848 | tf_op jit(solution)/shard_map/ppermute | solution.py:255
  210.9 17.1 %collective-permute-start.49 = (bf16[2,64,2880]{2,1,0:T(8,128)(2,1)}, bf16[2,64,2880]{2,1,0:T(8,128)(2,1)S(1)}, u32[]{:S(2)}, u32[]{:S(2)}) collective-permute-start(bf16[2,64,2880]{2,1,0:T(8,128)(2,1)} %pad_maximum_fusion.15), channel_id=1, source_target_pairs={{0,4},{1,3},{2,6},{3,1},{4,0},{5,7},{6,2},{7,5},{8,12},{9,11},{10,... | collective-permute-start | bytes 2211848 | tf_op jit(solution)/shard_map/ppermute | solution.py:263
  225.9 11.8 %collective-permute-start.35 = (bf16[2880,128]{1,0:T(8,128)(2,1)}, bf16[2880,128]{1,0:T(8,128)(2,1)}, u32[]{:S(2)}, u32[]{:S(2)}) collective-permute-start(bf16[2880,128]{1,0:T(8,128)(2,1)} %get-tuple-element.113), channel_id=1, source_target_pairs={{0,2},{1,5},{2,0},{3,7},{4,6},{5,1},{6,4},{7,3},{8,10},{9,13},{10,... | collective-permute-start | bytes 2211848 | tf_op jit(solution)/shard_map/ppermute | solution.py:259
  232.3 19.7 %collective-permute-start.50 = (bf16[2880,128]{1,0:T(8,128)(2,1)}, bf16[2880,128]{1,0:T(8,128)(2,1)S(1)}, u32[]{:S(2)}, u32[]{:S(2)}) collective-permute-start(bf16[2880,128]{1,0:T(8,128)(2,1)} %get-tuple-element.136), channel_id=1, source_target_pairs={{0,2},{1,5},{2,0},{3,7},{4,6},{5,1},{6,4},{7,3},{8,10},{9,13},{10,... | collective-permute-start | bytes 2211848 | tf_op jit(solution)/shard_map/ppermute | solution.py:259
  237.7 15.8 %collective-permute-start.36 = (bf16[2,64,2880]{2,1,0:T(8,128)(2,1)S(1)}, bf16[2,64,2880]{2,1,0:T(8,128)(2,1)S(1)}, u32[]{:S(2)}, u32[]{:S(2)}) collective-permute-start(bf16[2,64,2880]{2,1,0:T(8,128)(2,1)S(1)} %pad_maximum_fusion.10), channel_id=1, source_target_pairs={{0,4},{1,3},{2,6},{3,1},{4,0},{5,7},{6,2},{7,5},{8,12},{9,11},{10,... | collective-permute-start | bytes 2211848 | tf_op jit(solution)/shard_map/ppermute | solution.py:263
  241.4 30.8 %collective-permute-start.42 = (bf16[2880,128]{1,0:T(8,128)(2,1)}, bf16[2880,128]{1,0:T(8,128)(2,1)}, u32[]{:S(2)}, u32[]{:S(2)}) collective-permute-start(bf16[2880,128]{1,0:T(8,128)(2,1)} %add_convert_fusion.7), channel_id=1, source_target_pairs={{0,24},{1,25},{2,26},{3,27},{4,28},{5,29},{6,30},{7,31},{8,0},{9,1... | collective-permute-start | bytes 2211848 | tf_op jit(solution)/shard_map/ppermute | solution.py:267
  252.0 12.7 %collective-permute-start.51 = (bf16[2,64,2880]{2,1,0:T(8,128)(2,1)S(1)}, bf16[2,64,2880]{2,1,0:T(8,128)(2,1)S(1)}, u32[]{:S(2)}, u32[]{:S(2)}) collective-permute-start(bf16[2,64,2880]{2,1,0:T(8,128)(2,1)S(1)} %pad_maximum_fusion.14), channel_id=1, source_target_pairs={{0,4},{1,3},{2,6},{3,1},{4,0},{5,7},{6,2},{7,5},{8,12},{9,11},{10,... | collective-permute-start | bytes 2211848 | tf_op jit(solution)/shard_map/ppermute | solution.py:263
  259.5 11.8 %collective-permute-start.37 = (bf16[2880,128]{1,0:T(8,128)(2,1)}, bf16[2880,128]{1,0:T(8,128)(2,1)}, u32[]{:S(2)}, u32[]{:S(2)}) collective-permute-start(bf16[2880,128]{1,0:T(8,128)(2,1)} %get-tuple-element.115), channel_id=1, source_target_pairs={{0,2},{1,5},{2,0},{3,7},{4,6},{5,1},{6,4},{7,3},{8,10},{9,13},{10,... | collective-permute-start | bytes 2211848 | tf_op jit(solution)/shard_map/ppermute | solution.py:259
  261.1 34.5 %collective-permute-start.57 = (bf16[2880,128]{1,0:T(8,128)(2,1)}, bf16[2880,128]{1,0:T(8,128)(2,1)S(1)}, u32[]{:S(2)}, u32[]{:S(2)}) collective-permute-start(bf16[2880,128]{1,0:T(8,128)(2,1)} %add_convert_fusion.3), channel_id=1, source_target_pairs={{0,24},{1,25},{2,26},{3,27},{4,28},{5,29},{6,30},{7,31},{8,0},{9,1... | collective-permute-start | bytes 2211848 | tf_op jit(solution)/shard_map/ppermute | solution.py:267
  269.0 18.1 %collective-permute-start.52 = (bf16[2880,128]{1,0:T(8,128)(2,1)}, bf16[2880,128]{1,0:T(8,128)(2,1)S(1)}, u32[]{:S(2)}, u32[]{:S(2)}) collective-permute-start(bf16[2880,128]{1,0:T(8,128)(2,1)} %get-tuple-element.138), channel_id=1, source_target_pairs={{0,2},{1,5},{2,0},{3,7},{4,6},{5,1},{6,4},{7,3},{8,10},{9,13},{10,... | collective-permute-start | bytes 2211848 | tf_op jit(solution)/shard_map/ppermute | solution.py:259
  271.3 17.2 %collective-permute-start.38 = (bf16[2,64,2880]{2,1,0:T(8,128)(2,1)S(1)}, bf16[2,64,2880]{2,1,0:T(8,128)(2,1)S(1)}, u32[]{:S(2)}, u32[]{:S(2)}) collective-permute-start(bf16[2,64,2880]{2,1,0:T(8,128)(2,1)S(1)} %pad_maximum_fusion.9), channel_id=1, source_target_pairs={{0,4},{1,3},{2,6},{3,1},{4,0},{5,7},{6,2},{7,5},{8,12},{9,11},{10,... | collective-permute-start | bytes 2211848 | tf_op jit(solution)/shard_map/ppermute | solution.py:263
  273.7 33.6 %collective-permute-start.43 = (bf16[2880,128]{1,0:T(8,128)(2,1)S(1)}, bf16[2880,128]{1,0:T(8,128)(2,1)}, u32[]{:S(2)}, u32[]{:S(2)}) collective-permute-start(bf16[2880,128]{1,0:T(8,128)(2,1)S(1)} %add_convert_fusion.6), channel_id=1, source_target_pairs={{0,24},{1,25},{2,26},{3,27},{4,28},{5,29},{6,30},{7,31},{8,0},{9,1... | collective-permute-start | bytes 2211848 | tf_op jit(solution)/shard_map/ppermute | solution.py:267
  287.1 13.6 %collective-permute-start.53 = (bf16[2,64,2880]{2,1,0:T(8,128)(2,1)S(1)}, bf16[2,64,2880]{2,1,0:T(8,128)(2,1)S(1)}, u32[]{:S(2)}, u32[]{:S(2)}) collective-permute-start(bf16[2,64,2880]{2,1,0:T(8,128)(2,1)S(1)} %pad_maximum_fusion.13), channel_id=1, source_target_pairs={{0,4},{1,3},{2,6},{3,1},{4,0},{5,7},{6,2},{7,5},{8,12},{9,11},{10,... | collective-permute-start | bytes 2211848 | tf_op jit(solution)/shard_map/ppermute | solution.py:263
  294.4 12.7 %collective-permute-start.39 = (bf16[2880,128]{1,0:T(8,128)(2,1)}, bf16[2880,128]{1,0:T(8,128)(2,1)}, u32[]{:S(2)}, u32[]{:S(2)}) collective-permute-start(bf16[2880,128]{1,0:T(8,128)(2,1)} %get-tuple-element.117), channel_id=1, source_target_pairs={{0,2},{1,5},{2,0},{3,7},{4,6},{5,1},{6,4},{7,3},{8,10},{9,13},{10,... | collective-permute-start | bytes 2211848 | tf_op jit(solution)/shard_map/ppermute | solution.py:259
  297.9 35.4 %collective-permute-start.58 = (bf16[2880,128]{1,0:T(8,128)(2,1)S(1)}, bf16[2880,128]{1,0:T(8,128)(2,1)S(1)}, u32[]{:S(2)}, u32[]{:S(2)}) collective-permute-start(bf16[2880,128]{1,0:T(8,128)(2,1)S(1)} %add_convert_fusion.2), channel_id=1, source_target_pairs={{0,24},{1,25},{2,26},{3,27},{4,28},{5,29},{6,30},{7,31},{8,0},{9,1... | collective-permute-start | bytes 2211848 | tf_op jit(solution)/shard_map/ppermute | solution.py:267
  305.0 18.7 %collective-permute-start.54 = (bf16[2880,128]{1,0:T(8,128)(2,1)}, bf16[2880,128]{1,0:T(8,128)(2,1)}, u32[]{:S(2)}, u32[]{:S(2)}) collective-permute-start(bf16[2880,128]{1,0:T(8,128)(2,1)} %get-tuple-element.140), channel_id=1, source_target_pairs={{0,2},{1,5},{2,0},{3,7},{4,6},{5,1},{6,4},{7,3},{8,10},{9,13},{10,... | collective-permute-start | bytes 2211848 | tf_op jit(solution)/shard_map/ppermute | solution.py:259
  307.1 17.6 %collective-permute-start.40 = (bf16[2,64,2880]{2,1,0:T(8,128)(2,1)S(1)}, bf16[2,64,2880]{2,1,0:T(8,128)(2,1)S(1)}, u32[]{:S(2)}, u32[]{:S(2)}) collective-permute-start(bf16[2,64,2880]{2,1,0:T(8,128)(2,1)S(1)} %pad_maximum_fusion.8), channel_id=1, source_target_pairs={{0,4},{1,3},{2,6},{3,1},{4,0},{5,7},{6,2},{7,5},{8,12},{9,11},{10,... | collective-permute-start | bytes 2211848 | tf_op jit(solution)/shard_map/ppermute | solution.py:263
  308.9 37.1 %collective-permute-start.44 = (bf16[2880,128]{1,0:T(8,128)(2,1)S(1)}, bf16[2880,128]{1,0:T(8,128)(2,1)S(1)}, u32[]{:S(2)}, u32[]{:S(2)}) collective-permute-start(bf16[2880,128]{1,0:T(8,128)(2,1)S(1)} %add_convert_fusion.5), channel_id=1, source_target_pairs={{0,24},{1,25},{2,26},{3,27},{4,28},{5,29},{6,30},{7,31},{8,0},{9,1... | collective-permute-start | bytes 2211848 | tf_op jit(solution)/shard_map/ppermute | solution.py:267
  323.7 13.3 %collective-permute-start.55 = (bf16[2,64,2880]{2,1,0:T(8,128)(2,1)S(1)}, bf16[2,64,2880]{2,1,0:T(8,128)(2,1)S(1)}, u32[]{:S(2)}, u32[]{:S(2)}) collective-permute-start(bf16[2,64,2880]{2,1,0:T(8,128)(2,1)S(1)} %pad_maximum_fusion.12), channel_id=1, source_target_pairs={{0,4},{1,3},{2,6},{3,1},{4,0},{5,7},{6,2},{7,5},{8,12},{9,11},{10,... | collective-permute-start | bytes 2211848 | tf_op jit(solution)/shard_map/ppermute | solution.py:263
  332.7 13.3 %collective-permute-start.41 = (bf16[2880,128]{1,0:T(8,128)(2,1)}, bf16[2880,128]{1,0:T(8,128)(2,1)S(1)}, u32[]{:S(2)}, u32[]{:S(2)}) collective-permute-start(bf16[2880,128]{1,0:T(8,128)(2,1)} %get-tuple-element.120), channel_id=1, source_target_pairs={{0,2},{1,5},{2,0},{3,7},{4,6},{5,1},{6,4},{7,3},{8,10},{9,13},{10,... | collective-permute-start | bytes 2211848 | tf_op jit(solution)/shard_map/ppermute | solution.py:259
  341.4 18.7 %collective-permute-start.59 = (bf16[2880,128]{1,0:T(8,128)(2,1)S(1)}, bf16[2880,128]{1,0:T(8,128)(2,1)S(1)}, u32[]{:S(2)}, u32[]{:S(2)}) collective-permute-start(bf16[2880,128]{1,0:T(8,128)(2,1)S(1)} %add_convert_fusion.1), channel_id=1, source_target_pairs={{0,24},{1,25},{2,26},{3,27},{4,28},{5,29},{6,30},{7,31},{8,0},{9,1... | collective-permute-start | bytes 2211848 | tf_op jit(solution)/shard_map/ppermute | solution.py:267
  344.9 15.2 %collective-permute-start.56 = (bf16[2880,128]{1,0:T(8,128)(2,1)}, bf16[2880,128]{1,0:T(8,128)(2,1)S(1)}, u32[]{:S(2)}, u32[]{:S(2)}) collective-permute-start(bf16[2880,128]{1,0:T(8,128)(2,1)} %get-tuple-element.143), channel_id=1, source_target_pairs={{0,2},{1,5},{2,0},{3,7},{4,6},{5,1},{6,4},{7,3},{8,10},{9,13},{10,... | collective-permute-start | bytes 2211848 | tf_op jit(solution)/shard_map/ppermute | solution.py:259
  (89 other events, 474.1 us)

commit v2 on v1

--- a/solution.py
+++ b/solution.py
@@ -354,7 +354,11 @@
         )(pos, code_scales, *token_rows[span], *grad_rows[span], gate_codes, up_codes, down_codes)
         return done[: 3 * planes], done[3 * planes :]
 
-    parts, grads = run_experts((0, 1, 2, 3))
+    parts, grads = [], []
+    for steps in ((0, 1), (2, 3)):
+        more = run_experts(steps)
+        parts += more[0]
+        grads += more[1]
 
     own_type = jax.ShapeDtypeStruct((width, tok_rows), F32)
     other_type = jax.ShapeDtypeStruct((width, tok_rows), BF16)
@@ -362,10 +366,11 @@
 
     def gather(rows, outputs):
         total, routes, last = None, [None] * 4, []
-        for step in (3, 2, 1, 0):
+        for step in (1, 2, 3, 0):
             kept, far, core = rows[3 * step : 3 * step + 3]
             core = with_core(core)
             far = with_far(after(jnp.stack([far, core[1]]), *last))
+            last = [far]
             own, other, *route = pl.pallas_call(
                 functools.partial(combine_out_kernel if outputs else combine_kernel, slots, experts),
                 out_shape=[own_type, other_type] + [route_type] * outputs,
@@ -381,10 +386,9 @@
             )(pos, *infos[step], kept, core, far, *(raw_grads[step] if outputs else ()))
             routes[step] = route
             other = with_near(other)
-            last = [other]
             value = own + other.astype(F32)
             if total is not None:
-                value = value + to_next_plane(total, -1).astype(F32)
+                value = value + to_next_plane(total, 1).astype(F32)
             total = value.astype(BF16)
         return total, routes
 

time: 362 us -> 351 us (0.970); the launches traced: 361 us -> 344 us
  Pallas kernels: 101 us -> 123 us
  waiting for transfers between devices: 146 us -> 125 us
  starting transfers between devices: 70.5 us -> 57.5 us
  local copies, waits for them, and re-layouts: 23.6 us -> 15.9 us
    pallas_call x1 -> x2, Pallas kernels: 38.9 us -> 61.5 us  [run_experts(): pl.pallas_call(functools.partial(experts_kernel, experts, planes), out_sh...]
    ppermute x15, starting transfers between devices: 27.2 us -> 14.9 us  [to_next_plane(): lax.ppermute(value, AXES, [(n, (n + 8 * by) % 32) for n in range(32)])]
    ppermute x17, waiting for transfers between devices: 40.4 us -> 29.9 us  [with_near(): lax.ppermute(value, AXES, [(n, n ^ (ROW if n & CORE else COL)) for n in r...]
    ppermute x15, waiting for transfers between devices: 63.1 us -> 54.3 us  [to_next_plane(): lax.ppermute(value, AXES, [(n, (n + 8 * by) % 32) for n in range(32)])]
    unnamed x141 -> x133, local copies, waits for them, and re-layouts: 18.7 us -> 11.9 us
    ppermute x16, waiting for transfers between devices: 4.14 us -> 0.36 us  [with_core(): return lax.ppermute(value, AXES, [(n, n ^ CORE) for n in range(32)])]
  transfers between devices with their start and end apart: 64 -> 64, of which waited for: 29 -> 19; matrix products, arithmetic and copies ran while one was open for 6% -> 7% of each run, Pallas kernels for 17% -> 36%
where the time goes in v2:
time: 351 us; the launch traced here: 344 us
  waiting for transfers between devices  125 us (36%)
  Pallas kernels  123 us (35%)
  starting transfers between devices  57.5 us (16%)
  other arithmetic  20.7 us (6%)
  local copies, waits for them, and re-layouts  15.9 us (5%)
    pallas_call x2, Pallas kernels, run_experts(): pl.pallas_call(functools.partial(experts_kernel, experts, planes), out_sh...  61.5 us
    ppermute x15, waiting for transfers between devices, to_next_plane(): lax.ppermute(value, AXES, [(n, (n + 8 * by) % 32) for n in range(32)])  54.3 us
    ppermute x16, waiting for transfers between devices, with_far(): lax.ppermute(value, AXES, [(n, n ^ (COL if n & CORE else ROW)) for n in r...  40.7 us
    pallas_call x8, Pallas kernels, gather(): pl.pallas_call(functools.partial(combine_out_kernel if outputs else combi...  33.9 us
    ppermute x17, waiting for transfers between devices, with_near(): lax.ppermute(value, AXES, [(n, n ^ (ROW if n & CORE else COL)) for n in r...  29.9 us
    pallas_call x8, Pallas kernels, spread(): pl.pallas_call(functools.partial(pack_kernel, slots, experts, scaled), ou...  27.6 us
    ppermute x17, starting transfers between devices, with_near(): lax.ppermute(value, AXES, [(n, n ^ (ROW if n & CORE else COL)) for n in r...  19.2 us
    ppermute x16, starting transfers between devices, with_far(): lax.ppermute(value, AXES, [(n, n ^ (COL if n & CORE else ROW)) for n in r...  16.4 us
  transfers between devices with their start and end apart: 64, of which 19 were waited for; matrix products, arithmetic and copies ran while one was open for 7% of the time, Pallas kernels for 36%

profile of v2, /device:TPU:0, one launch (start us, length us, event | category | flops | bytes accessed | tf_op | source)
XLA Modules:
  0.0 344.3 jit_solution(16242595415744958595)
XLA Ops:
  0.6 3.1 collective-permute-start.10
  6.0 2.9 concatenate.6.own_info.own_ref
  8.9 1.6 collective-permute-start.3
  12.6 10.8 %collective-permute-done.10.own_ref.d_own_ref = bf16[2880,128]{1,0:T(8,128)(2,1)} collective-permute-done((bf16[2880,128]{1,0:T(8,128)(2,1)}, bf16[2880,128]{1,0:T(8,128)(2,1)}, u32[]{:S(2)}, u32[]{:S(2)}) %collective-permute-start.10) | collective-permute-done | bytes 737312 | tf_op jit(solution)/shard_map/ppermute | solution.py:267
  23.4 1.7 collective-permute-start.11
  25.1 13.2 %collective-permute-done.3.own_info.own_ref = bf16[2896,128]{1,0:T(8,128)(2,1)S(1)} collective-permute-done((bf16[2896,128]{1,0:T(8,128)(2,1)S(1)}, bf16[2896,128]{1,0:T(8,128)(2,1)S(1)}, u32[]{:S(2)}, u32[]{:S(2)}) %collective-permute-start.3) | collective-permute-done | bytes 741408 | tf_op jit(solution)/shard_map/ppermute | solution.py:267
  41.4 3.4 pack_gradients.4
  47.6 3.4 pack_tokens.4
  51.5 1.7 collective-permute-done.4.other_info.other_ref
  54.1 3.5 %pack_gradients.5 = (bf16[64,2880]{1,0:T(8,128)(2,1)}, bf16[64,2880]{1,0:T(8,128)(2,1)}, bf16[2,64,2880]{2,1,0:T(8,128)(2,1)}) custom-call(s32[2]{0:T(128)} %pad_add_fusion.pos_ref, bf16[2896,128]{1,0:T(8,128)(2,1)} %copy-done.6, bf16[2896,128]{1,0:T(8,128)(2,1)} %copy-done.7, bf16[2880,128]{1,0:T(8,128)(2,1)} %collective-permute-done.10.own_ref.d_own_ref, ...), custom_call_target="tpu_custom_call" | custom-call | flops 377487360 | bytes 2211840 | tf_op jit(solution)/shard_map/pack_gradients/pallas_call | solution.py:309
  57.6 2.3 collective-permute-start.12
  59.9 3.5 %pack_tokens.5 = (bf16[64,2880]{1,0:T(8,128)(2,1)}, bf16[64,2880]{1,0:T(8,128)(2,1)}, bf16[2,64,2880]{2,1,0:T(8,128)(2,1)}) custom-call(s32[2]{0:T(128)} %pad_add_fusion.pos_ref, bf16[2896,128]{1,0:T(8,128)(2,1)} %copy-done.6, bf16[2896,128]{1,0:T(8,128)(2,1)} %copy-done.7, bf16[2896,128]{1,0:T(8,128)(2,1)} %copy-done.6, bf16[2896,128]{1,0:T(8,128)(2,1)} %copy-done.7), custom_call_target="tpu_custom_call" | custom-call | flops 377487360 | bytes 2211840 | tf_op jit(solution)/shard_map/pack_tokens/pallas_call | solution.py:309
  64.7 1.7 collective-permute-start.24
  66.4 11.4 %collective-permute-done.15.own_info.own_ref = bf16[2896,128]{1,0:T(8,128)(2,1)S(1)} collective-permute-done((bf16[2896,128]{1,0:T(8,128)(2,1)S(1)}, bf16[2896,128]{1,0:T(8,128)(2,1)S(1)}, u32[]{:S(2)}, u32[]{:S(2)}) %collective-permute-start.15) | collective-permute-done | bytes 741408 | tf_op jit(solution)/shard_map/ppermute | solution.py:267
  78.4 1.6 collective-permute-start.9
  80.1 12.9 %collective-permute-done.5.refs_4_ = bf16[2,64,2880]{2,1,0:T(8,128)(2,1)S(1)} collective-permute-done((bf16[2,64,2880]{2,1,0:T(8,128)(2,1)}, bf16[2,64,2880]{2,1,0:T(8,128)(2,1)S(1)}, u32[]{:S(2)}, u32[]{:S(2)}) %collective-permute-start.5) | collective-permute-done | bytes 737312 | tf_op jit(solution)/shard_map/ppermute | solution.py:263
  92.9 3.1 collective-permute-start.2
  100.0 3.5 %pack_tokens.6 = (bf16[64,2880]{1,0:T(8,128)(2,1)}, bf16[64,2880]{1,0:T(8,128)(2,1)}, bf16[2,64,2880]{2,1,0:T(8,128)(2,1)}) custom-call(s32[2]{0:T(128)} %pad_add_fusion.pos_ref, bf16[2896,128]{1,0:T(8,128)(2,1)} %copy-done.2, bf16[2896,128]{1,0:T(8,128)(2,1)} %copy-done.4, bf16[2896,128]{1,0:T(8,128)(2,1)} %copy-done.2, bf16[2896,128]{1,0:T(8,128)(2,1)} %copy-done.4), custom_call_target="tpu_custom_call" | custom-call | flops 377487360 | bytes 2211840 | tf_op jit(solution)/shard_map/pack_tokens/pallas_call | solution.py:309
  103.4 3.5 %pack_gradients.6 = (bf16[64,2880]{1,0:T(8,128)(2,1)}, bf16[64,2880]{1,0:T(8,128)(2,1)}, bf16[2,64,2880]{2,1,0:T(8,128)(2,1)}) custom-call(s32[2]{0:T(128)} %pad_add_fusion.pos_ref, bf16[2896,128]{1,0:T(8,128)(2,1)} %copy-done.2, bf16[2896,128]{1,0:T(8,128)(2,1)} %copy-done.4, bf16[2880,128]{1,0:T(8,128)(2,1)} %copy-done.8, bf16[2880,128]{1,0:T(8,128)(2,1)} %copy-done.9), custom_call_target="tpu_custom_call" | custom-call | flops 377487360 | bytes 2211840 | tf_op jit(solution)/shard_map/pack_gradients/pallas_call | solution.py:309
  109.3 8.2 %collective-permute-done.19.own_info.own_ref = bf16[2896,128]{1,0:T(8,128)(2,1)S(1)} collective-permute-done((bf16[2896,128]{1,0:T(8,128)(2,1)S(1)}, bf16[2896,128]{1,0:T(8,128)(2,1)S(1)}, u32[]{:S(2)}, u32[]{:S(2)}) %collective-permute-start.19) | collective-permute-done | bytes 741408 | tf_op jit(solution)/shard_map/ppermute | solution.py:267
  119.9 30.7 %experts.2 = (bf16[64,2880]{1,0:T(8,128)(2,1)}, bf16[64,2880]{1,0:T(8,128)(2,1)}, bf16[2,64,2880]{2,1,0:T(8,128)(2,1)}, bf16[64,2880]{1,0:T(8,128)(2,1)}, bf16[6...) custom-call(s32[2]{0:T(128)} %pad_add_fusion.pos_ref, ...), custom_call_target="tpu_custom_call" | custom-call | flops 12740198400 | bytes 49766400 | tf_op jit(solution)/shard_map/experts/pallas_call | solution.py:339
  153.4 3.4 pack_gradients.7
  157.9 3.4 pack_tokens.7
  164.8 3.9 %collective-permute-done.29.refs_10_ = bf16[2,64,2880]{2,1,0:T(8,128)(2,1)S(1)} collective-permute-done((bf16[2,64,2880]{2,1,0:T(8,128)(2,1)}, bf16[2,64,2880]{2,1,0:T(8,128)(2,1)S(1)}, u32[]{:S(2)}, u32[]{:S(2)}) %collective-permute-start.29) | collective-permute-done | bytes 737312 | tf_op jit(solution)/shard_map/ppermute | solution.py:263
  168.7 8.0 %collective-permute-done.21.refs_4_ = bf16[2,64,2880]{2,1,0:T(8,128)(2,1)S(1)} collective-permute-done((bf16[2,64,2880]{2,1,0:T(8,128)(2,1)}, bf16[2,64,2880]{2,1,0:T(8,128)(2,1)S(1)}, u32[]{:S(2)}, u32[]{:S(2)}) %collective-permute-start.21) | collective-permute-done | bytes 737312 | tf_op jit(solution)/shard_map/ppermute | solution.py:263
  178.2 6.7 %collective-permute-done.34.far_ref = bf16[2,64,2880]{2,1,0:T(8,128)(2,1)S(1)} collective-permute-done((bf16[2,64,2880]{2,1,0:T(8,128)(2,1)S(1)}, bf16[2,64,2880]{2,1,0:T(8,128)(2,1)S(1)}, u32[]{:S(2)}, u32[]{:S(2)}) %collective-permute-start.34) | collective-permute-done | bytes 737312 | tf_op jit(solution)/shard_map/ppermute | solution.py:263
  186.0 5.0 %sum_outputs.7 = (f32[2880,128]{1,0:T(8,128)}, bf16[2880,128]{1,0:T(8,128)(2,1)}, f32[2,2,128]{2,1,0:T(2,128)}) custom-call(s32[2]{0:T(128)} %pad_add_fusion.pos_ref, bf16[2896,128]{1,0:T(8,128)(2,1)} %copy-done.6, bf16[2896,128]{1,0:T(8,128)(2,1)} %copy-done.7, bf16[64,2880]{1,0:T(8,128)(2,1)} %get-tuple-element.121.kept_ref, ...), custom_call_target="tpu_custom_call" | custom-call | flops 377487360 | bytes 2211840 | tf_op jit(solution)/shard_map/sum_outputs/pallas_call | solution.py:374
  191.0 2.0 collective-permute-done.49.far_ref
  193.8 3.3 sum_gradients.7
  198.4 30.8 %experts.3 = (bf16[64,2880]{1,0:T(8,128)(2,1)}, bf16[64,2880]{1,0:T(8,128)(2,1)}, bf16[2,64,2880]{2,1,0:T(8,128)(2,1)}, bf16[64,2880]{1,0:T(8,128)(2,1)}, bf16[6...) custom-call(s32[2]{0:T(128)} %pad_add_fusion.pos_ref, ...), custom_call_target="tpu_custom_call" | custom-call | flops 12740198400 | bytes 49766400 | tf_op jit(solution)/shard_map/experts/pallas_call | solution.py:339
  230.3 2.2 add_convert_fusion.7
  234.2 2.3 add_convert_fusion.3
  237.8 6.9 %collective-permute-done.35.far_ref = bf16[2,64,2880]{2,1,0:T(8,128)(2,1)S(1)} collective-permute-done((bf16[2,64,2880]{2,1,0:T(8,128)(2,1)S(1)}, bf16[2,64,2880]{2,1,0:T(8,128)(2,1)S(1)}, u32[]{:S(2)}, u32[]{:S(2)}) %collective-permute-start.35) | collective-permute-done | bytes 737312 | tf_op jit(solution)/shard_map/ppermute | solution.py:263
  245.6 5.1 %sum_outputs.6 = (f32[2880,128]{1,0:T(8,128)}, bf16[2880,128]{1,0:T(8,128)(2,1)}, f32[2,2,128]{2,1,0:T(2,128)}) custom-call(s32[2]{0:T(128)} %pad_add_fusion.pos_ref, bf16[2896,128]{1,0:T(8,128)(2,1)} %copy-done.2, bf16[2896,128]{1,0:T(8,128)(2,1)} %copy-done.4, bf16[64,2880]{1,0:T(8,128)(2,1)} %get-tuple-element.118.kept_ref, ...), custom_call_target="tpu_custom_call" | custom-call | flops 377487360 | bytes 2211840 | tf_op jit(solution)/shard_map/sum_outputs/pallas_call | solution.py:374
  253.8 3.5 %sum_gradients.6 = (f32[2880,128]{1,0:T(8,128)}, bf16[2880,128]{1,0:T(8,128)(2,1)}) custom-call(s32[2]{0:T(128)} %pad_add_fusion.pos_ref, bf16[2896,128]{1,0:T(8,128)(2,1)} %copy-done.2, bf16[2896,128]{1,0:T(8,128)(2,1)} %copy-done.4, bf16[64,2880]{1,0:T(8,128)(2,1)} %get-tuple-element.141.kept_ref, bf16[2,64,2880]{2,1,0:T(8,128)(2,1)} %copy-done.17, ...), custom_call_target="tpu_custom_call" | custom-call | flops 377487360 | bytes 2211840 | tf_op jit(solution)/shard_map/sum_gradients/pallas_call | solution.py:374
  259.5 10.8 %collective-permute-done.40 = bf16[2880,128]{1,0:T(8,128)(2,1)} collective-permute-done((bf16[2880,128]{1,0:T(8,128)(2,1)}, bf16[2880,128]{1,0:T(8,128)(2,1)}, u32[]{:S(2)}, u32[]{:S(2)}) %collective-permute-start.40) | collective-permute-done | bytes 737312 | tf_op jit(solution)/shard_map/ppermute | solution.py:259
  270.4 2.4 add_convert_fusion.6
  273.9 5.1 %sum_outputs.5 = (f32[2880,128]{1,0:T(8,128)}, bf16[2880,128]{1,0:T(8,128)(2,1)}, f32[2,2,128]{2,1,0:T(2,128)}) custom-call(s32[2]{0:T(128)} %pad_add_fusion.pos_ref, bf16[2896,128]{1,0:T(8,128)(2,1)} %copy-done.3, bf16[2896,128]{1,0:T(8,128)(2,1)} %copy-done.5, bf16[64,2880]{1,0:T(8,128)(2,1)} %get-tuple-element.115.kept_ref, ...), custom_call_target="tpu_custom_call" | custom-call | flops 377487360 | bytes 2211840 | tf_op jit(solution)/shard_map/sum_outputs/pallas_call | solution.py:374
  280.7 5.3 %collective-permute-done.55 = bf16[2880,128]{1,0:T(8,128)(2,1)S(1)} collective-permute-done((bf16[2880,128]{1,0:T(8,128)(2,1)}, bf16[2880,128]{1,0:T(8,128)(2,1)S(1)}, u32[]{:S(2)}, u32[]{:S(2)}) %collective-permute-start.55) | collective-permute-done | bytes 737312 | tf_op jit(solution)/shard_map/ppermute | solution.py:259
  289.6 3.5 %sum_gradients.5 = (f32[2880,128]{1,0:T(8,128)}, bf16[2880,128]{1,0:T(8,128)(2,1)}) custom-call(s32[2]{0:T(128)} %pad_add_fusion.pos_ref, bf16[2896,128]{1,0:T(8,128)(2,1)} %copy-done.3, bf16[2896,128]{1,0:T(8,128)(2,1)} %copy-done.5, bf16[64,2880]{1,0:T(8,128)(2,1)} %get-tuple-element.138.kept_ref, bf16[2,64,2880]{2,1,0:T(8,128)(2,1)} %copy-done.13, ...), custom_call_target="tpu_custom_call" | custom-call | flops 377487360 | bytes 2211840 | tf_op jit(solution)/shard_map/sum_gradients/pallas_call | solution.py:374
  294.9 7.0 %collective-permute-done.39 = bf16[2880,128]{1,0:T(8,128)(2,1)} collective-permute-done((bf16[2880,128]{1,0:T(8,128)(2,1)}, bf16[2880,128]{1,0:T(8,128)(2,1)}, u32[]{:S(2)}, u32[]{:S(2)}) %collective-permute-start.39) | collective-permute-done | bytes 737312 | tf_op jit(solution)/shard_map/ppermute | solution.py:259
  302.0 1.6 add_convert_fusion.5
  304.9 5.1 %sum_outputs.4 = (f32[2880,128]{1,0:T(8,128)}, bf16[2880,128]{1,0:T(8,128)(2,1)}, f32[2,2,128]{2,1,0:T(2,128)}) custom-call(s32[2]{0:T(128)} %pad_add_fusion.pos_ref, bf16[2896,128]{1,0:T(8,128)(2,1)} %copy-done, bf16[2896,128]{1,0:T(8,128)(2,1)} %copy-done.1, bf16[64,2880]{1,0:T(8,128)(2,1)} %get-tuple-element.89.kept_ref, bf16[2,64,2880]{2,1,0:T(8,128)(2,1)} %copy-done.12, ...), custom_call_target="tpu_custom_call" | custom-call | flops 377487360 | bytes 2211840 | tf_op jit(solution)/shard_map/sum_outputs/pallas_call | solution.py:374
  312.7 5.0 %collective-permute-done.54 = bf16[2880,128]{1,0:T(8,128)(2,1)S(1)} collective-permute-done((bf16[2880,128]{1,0:T(8,128)(2,1)}, bf16[2880,128]{1,0:T(8,128)(2,1)S(1)}, u32[]{:S(2)}, u32[]{:S(2)}) %collective-permute-start.54) | collective-permute-done | bytes 737312 | tf_op jit(solution)/shard_map/ppermute | solution.py:259
  317.9 3.6 %collective-permute-start.61 = (f32[2,128]{1,0:T(2,128)S(1)}, f32[2,128]{1,0:T(2,128)S(1)}, u32[]{:S(2)}, u32[]{:S(2)}) collective-permute-start(f32[2,128]{1,0:T(2,128)S(1)} %get-tuple-element.151), channel_id=1, source_target_pairs={{0,24},{1,25},{2,26},{3,27},{4,28},{5,29},{6,30},{7,31},{8,0},{9,1... | collective-permute-start | bytes 3080 | tf_op jit(solution)/shard_map/ppermute | solution.py:267
  322.5 3.5 %sum_gradients.4 = (f32[2880,128]{1,0:T(8,128)}, bf16[2880,128]{1,0:T(8,128)(2,1)}) custom-call(s32[2]{0:T(128)} %pad_add_fusion.pos_ref, bf16[2896,128]{1,0:T(8,128)(2,1)} %copy-done, bf16[2896,128]{1,0:T(8,128)(2,1)} %copy-done.1, bf16[64,2880]{1,0:T(8,128)(2,1)} %get-tuple-element.124.kept_ref, bf16[2,64,2880]{2,1,0:T(8,128)(2,1)} %copy-done.11, ...), custom_call_target="tpu_custom_call" | custom-call | flops 377487360 | bytes 2211840 | tf_op jit(solution)/shard_map/sum_gradients/pallas_call | solution.py:374
  325.9 3.5 %collective-permute-start.59 = (bf16[2880,128]{1,0:T(8,128)(2,1)S(1)}, bf16[2880,128]{1,0:T(8,128)(2,1)S(1)}, u32[]{:S(2)}, u32[]{:S(2)}) collective-permute-start(bf16[2880,128]{1,0:T(8,128)(2,1)S(1)} %add_convert_fusion.1), channel_id=1, source_target_pairs={{0,8},{1,9},{2,10},{3,11},{4,12},{5,13},{6,14},{7,15},{8,16},{9,17... | collective-permute-start | bytes 2211848 | tf_op jit(solution)/shard_map/ppermute | solution.py:267
  332.0 10.6 %collective-permute-done.59 = bf16[2880,128]{1,0:T(8,128)(2,1)S(1)} collective-permute-done((bf16[2880,128]{1,0:T(8,128)(2,1)S(1)}, bf16[2880,128]{1,0:T(8,128)(2,1)S(1)}, u32[]{:S(2)}, u32[]{:S(2)}) %collective-permute-start.59) | collective-permute-done | bytes 737312 | tf_op jit(solution)/shard_map/ppermute | solution.py:267
  (289 shorter events, 61.2 us)
Async XLA Ops:
  0.6 22.7 %collective-permute-start.10 = (bf16[2880,128]{1,0:T(8,128)(2,1)}, bf16[2880,128]{1,0:T(8,128)(2,1)}, u32[]{:S(2)}, u32[]{:S(2)}) collective-permute-start(bf16[2880,128]{1,0:T(8,128)(2,1)} %bitcast.7.own_ref.d_own_ref), channel_id=1, source_target_pairs={{0,8},{1,9},{2,10},{3,11},{4,12},{5,13},{6,14},{7,15},{8,16},{9,17... | collective-permute-start | bytes 2211848 | tf_op jit(solution)/shard_map/ppermute | solution.py:267
  8.9 29.4 %collective-permute-start.3 = (bf16[2896,128]{1,0:T(8,128)(2,1)S(1)}, bf16[2896,128]{1,0:T(8,128)(2,1)S(1)}, u32[]{:S(2)}, u32[]{:S(2)}) collective-permute-start(bf16[2896,128]{1,0:T(8,128)(2,1)S(1)} %concatenate.6.own_info.own_ref), channel_id=1, source_target_pairs={{0,8},{1,9},{2,10},{3,11},{4,12},{5,13},{6,14},{7,15},{8,16},{9,17... | collective-permute-start | bytes 2224136 | tf_op jit(solution)/shard_map/ppermute | solution.py:267
  10.5 29.9 %collective-permute-start = (bf16[2896,128]{1,0:T(8,128)(2,1)S(1)}, bf16[2896,128]{1,0:T(8,128)(2,1)S(1)}, u32[]{:S(2)}, u32[]{:S(2)}) collective-permute-start(bf16[2896,128]{1,0:T(8,128)(2,1)S(1)} %concatenate.6.own_info.own_ref), channel_id=1, source_target_pairs={{0,2},{1,5},{2,0},{3,7},{4,6},{5,1},{6,4},{7,3},{8,10},{9,13},{10,... | collective-permute-start | bytes 2224136 | tf_op jit(solution)/shard_map/ppermute | solution.py:259
  12.0 28.4 %collective-permute-start.7 = (bf16[2880,128]{1,0:T(8,128)(2,1)}, bf16[2880,128]{1,0:T(8,128)(2,1)}, u32[]{:S(2)}, u32[]{:S(2)}) collective-permute-start(bf16[2880,128]{1,0:T(8,128)(2,1)} %bitcast.7.own_ref.d_own_ref), channel_id=1, source_target_pairs={{0,2},{1,5},{2,0},{3,7},{4,6},{5,1},{6,4},{7,3},{8,10},{9,13},{10,... | collective-permute-start | bytes 2211848 | tf_op jit(solution)/shard_map/ppermute | solution.py:259
  23.4 27.6 %collective-permute-start.11 = (bf16[2880,128]{1,0:T(8,128)(2,1)}, bf16[2880,128]{1,0:T(8,128)(2,1)}, u32[]{:S(2)}, u32[]{:S(2)}) collective-permute-start(bf16[2880,128]{1,0:T(8,128)(2,1)} %collective-permute-done.10.own_ref.d_own_ref), channel_id=1, source_target_pairs={{0,2},{1,5},{2,0},{3,7},{4,6},{5,1},{6,4},{7,3},{8,10},{9,13},{10,... | collective-permute-start | bytes 2211848 | tf_op jit(solution)/shard_map/ppermute | solution.py:259
  40.5 22.9 %collective-permute-start.23 = (bf16[2880,128]{1,0:T(8,128)(2,1)}, bf16[2880,128]{1,0:T(8,128)(2,1)S(1)}, u32[]{:S(2)}, u32[]{:S(2)}) collective-permute-start(bf16[2880,128]{1,0:T(8,128)(2,1)} %collective-permute-done.10.own_ref.d_own_ref), channel_id=1, source_target_pairs={{0,8},{1,9},{2,10},{3,11},{4,12},{5,13},{6,14},{7,15},{8,16},{9,17... | collective-permute-start | bytes 2211848 | tf_op jit(solution)/shard_map/ppermute | solution.py:267
  44.8 18.7 %collective-permute-start.8 = (bf16[2,64,2880]{2,1,0:T(8,128)(2,1)}, bf16[2,64,2880]{2,1,0:T(8,128)(2,1)S(1)}, u32[]{:S(2)}, u32[]{:S(2)}) collective-permute-start(bf16[2,64,2880]{2,1,0:T(8,128)(2,1)} %get-tuple-element.84), channel_id=1, source_target_pairs={{0,4},{1,3},{2,6},{3,1},{4,0},{5,7},{6,2},{7,5},{8,12},{9,11},{10,... | collective-permute-start | bytes 2211848 | tf_op jit(solution)/shard_map/ppermute | solution.py:263
  46.3 31.5 %collective-permute-start.15 = (bf16[2896,128]{1,0:T(8,128)(2,1)S(1)}, bf16[2896,128]{1,0:T(8,128)(2,1)S(1)}, u32[]{:S(2)}, u32[]{:S(2)}) collective-permute-start(bf16[2896,128]{1,0:T(8,128)(2,1)S(1)} %collective-permute-done.3.own_info.own_ref), channel_id=1, source_target_pairs={{0,8},{1,9},{2,10},{3,11},{4,12},{5,13},{6,14},{7,15},{8,16},{9,17... | collective-permute-start | bytes 2224136 | tf_op jit(solution)/shard_map/ppermute | solution.py:267
  57.6 20.8 %collective-permute-start.12 = (bf16[2,64,2880]{2,1,0:T(8,128)(2,1)}, bf16[2,64,2880]{2,1,0:T(8,128)(2,1)S(1)}, u32[]{:S(2)}, u32[]{:S(2)}) collective-permute-start(bf16[2,64,2880]{2,1,0:T(8,128)(2,1)} %get-tuple-element.87), channel_id=1, source_target_pairs={{0,4},{1,3},{2,6},{3,1},{4,0},{5,7},{6,2},{7,5},{8,12},{9,11},{10,... | collective-permute-start | bytes 2211848 | tf_op jit(solution)/shard_map/ppermute | solution.py:263
  63.4 29.6 %collective-permute-start.5 = (bf16[2,64,2880]{2,1,0:T(8,128)(2,1)}, bf16[2,64,2880]{2,1,0:T(8,128)(2,1)S(1)}, u32[]{:S(2)}, u32[]{:S(2)}) collective-permute-start(bf16[2,64,2880]{2,1,0:T(8,128)(2,1)} %get-tuple-element.81), channel_id=1, source_target_pairs={{0,4},{1,3},{2,6},{3,1},{4,0},{5,7},{6,2},{7,5},{8,12},{9,11},{10,... | collective-permute-start | bytes 2211848 | tf_op jit(solution)/shard_map/ppermute | solution.py:263
  63.5 33.6 %collective-permute-start.27 = (bf16[2880,128]{1,0:T(8,128)(2,1)S(1)}, bf16[2880,128]{1,0:T(8,128)(2,1)}, u32[]{:S(2)}, u32[]{:S(2)}) collective-permute-start(bf16[2880,128]{1,0:T(8,128)(2,1)S(1)} %collective-permute-done.23.own_ref.d_own_ref), channel_id=1, source_target_pairs={{0,8},{1,9},{2,10},{3,11},{4,12},{5,13},{6,14},{7,15},{8,16},{9,17... | collective-permute-start | bytes 2211848 | tf_op jit(solution)/shard_map/ppermute | solution.py:267
  64.7 33.4 %collective-permute-start.24 = (bf16[2880,128]{1,0:T(8,128)(2,1)S(1)}, bf16[2880,128]{1,0:T(8,128)(2,1)S(1)}, u32[]{:S(2)}, u32[]{:S(2)}) collective-permute-start(bf16[2880,128]{1,0:T(8,128)(2,1)S(1)} %collective-permute-done.23.own_ref.d_own_ref), channel_id=1, source_target_pairs={{0,2},{1,5},{2,0},{3,7},{4,6},{5,1},{6,4},{7,3},{8,10},{9,13},{10,... | collective-permute-start | bytes 2211848 | tf_op jit(solution)/shard_map/ppermute | solution.py:259
  77.8 20.5 %collective-permute-start.16 = (bf16[2896,128]{1,0:T(8,128)(2,1)S(1)}, bf16[2896,128]{1,0:T(8,128)(2,1)S(1)}, u32[]{:S(2)}, u32[]{:S(2)}) collective-permute-start(bf16[2896,128]{1,0:T(8,128)(2,1)S(1)} %collective-permute-done.15.own_info.own_ref), channel_id=1, source_target_pairs={{0,2},{1,5},{2,0},{3,7},{4,6},{5,1},{6,4},{7,3},{8,10},{9,13},{10,... | collective-permute-start | bytes 2224136 | tf_op jit(solution)/shard_map/ppermute | solution.py:259
  78.4 28.5 %collective-permute-start.9 = (bf16[2,64,2880]{2,1,0:T(8,128)(2,1)}, bf16[2,64,2880]{2,1,0:T(8,128)(2,1)}, u32[]{:S(2)}, u32[]{:S(2)}) collective-permute-start(bf16[2,64,2880]{2,1,0:T(8,128)(2,1)} %pad_maximum_fusion.2), channel_id=1, source_target_pairs={{0,1},{1,0},{2,3},{3,2},{4,5},{5,4},{6,7},{7,6},{8,9},{9,8},{10,11... | collective-permute-start | bytes 2211848 | tf_op jit(solution)/shard_map/ppermute | solution.py:255
  92.9 15.4 %collective-permute-start.2 = (bf16[2,64,2880]{2,1,0:T(8,128)(2,1)S(1)}, bf16[2,64,2880]{2,1,0:T(8,128)(2,1)}, u32[]{:S(2)}, u32[]{:S(2)}) collective-permute-start(bf16[2,64,2880]{2,1,0:T(8,128)(2,1)S(1)} %pad_maximum_fusion), channel_id=1, source_target_pairs={{0,1},{1,0},{2,3},{3,2},{4,5},{5,4},{6,7},{7,6},{8,9},{9,8},{10,11... | collective-permute-start | bytes 2211848 | tf_op jit(solution)/shard_map/ppermute | solution.py:255
  97.1 20.4 %collective-permute-start.19 = (bf16[2896,128]{1,0:T(8,128)(2,1)S(1)}, bf16[2896,128]{1,0:T(8,128)(2,1)S(1)}, u32[]{:S(2)}, u32[]{:S(2)}) collective-permute-start(bf16[2896,128]{1,0:T(8,128)(2,1)S(1)} %collective-permute-done.15.own_info.own_ref), channel_id=1, source_target_pairs={{0,8},{1,9},{2,10},{3,11},{4,12},{5,13},{6,14},{7,15},{8,16},{9,17... | collective-permute-start | bytes 2224136 | tf_op jit(solution)/shard_map/ppermute | solution.py:267
  98.1 20.5 %collective-permute-start.13 = (bf16[2,64,2880]{2,1,0:T(8,128)(2,1)}, bf16[2,64,2880]{2,1,0:T(8,128)(2,1)}, u32[]{:S(2)}, u32[]{:S(2)}) collective-permute-start(bf16[2,64,2880]{2,1,0:T(8,128)(2,1)} %pad_maximum_fusion.3), channel_id=1, source_target_pairs={{0,1},{1,0},{2,3},{3,2},{4,5},{5,4},{6,7},{7,6},{8,9},{9,8},{10,11... | collective-permute-start | bytes 2211848 | tf_op jit(solution)/shard_map/ppermute | solution.py:255
  99.1 20.8 %collective-permute-start.6 = (bf16[2,64,2880]{2,1,0:T(8,128)(2,1)}, bf16[2,64,2880]{2,1,0:T(8,128)(2,1)}, u32[]{:S(2)}, u32[]{:S(2)}) collective-permute-start(bf16[2,64,2880]{2,1,0:T(8,128)(2,1)} %pad_maximum_fusion.1), channel_id=1, source_target_pairs={{0,1},{1,0},{2,3},{3,2},{4,5},{5,4},{6,7},{7,6},{8,9},{9,8},{10,11... | collective-permute-start | bytes 2211848 | tf_op jit(solution)/shard_map/ppermute | solution.py:255
  106.9 44.7 %collective-permute-start.28 = (bf16[2880,128]{1,0:T(8,128)(2,1)}, bf16[2880,128]{1,0:T(8,128)(2,1)S(1)}, u32[]{:S(2)}, u32[]{:S(2)}) collective-permute-start(bf16[2880,128]{1,0:T(8,128)(2,1)} %collective-permute-done.27.own_ref.d_own_ref), channel_id=1, source_target_pairs={{0,2},{1,5},{2,0},{3,7},{4,6},{5,1},{6,4},{7,3},{8,10},{9,13},{10,... | collective-permute-start | bytes 2211848 | tf_op jit(solution)/shard_map/ppermute | solution.py:259
  108.3 42.4 %collective-permute-start.25 = (bf16[2,64,2880]{2,1,0:T(8,128)(2,1)}, bf16[2,64,2880]{2,1,0:T(8,128)(2,1)S(1)}, u32[]{:S(2)}, u32[]{:S(2)}) collective-permute-start(bf16[2,64,2880]{2,1,0:T(8,128)(2,1)} %get-tuple-element.99), channel_id=1, source_target_pairs={{0,4},{1,3},{2,6},{3,1},{4,0},{5,7},{6,2},{7,5},{8,12},{9,11},{10,... | collective-permute-start | bytes 2211848 | tf_op jit(solution)/shard_map/ppermute | solution.py:263
  117.5 33.6 %collective-permute-start.17 = (bf16[2,64,2880]{2,1,0:T(8,128)(2,1)S(1)}, bf16[2,64,2880]{2,1,0:T(8,128)(2,1)S(1)}, u32[]{:S(2)}, u32[]{:S(2)}) collective-permute-start(bf16[2,64,2880]{2,1,0:T(8,128)(2,1)S(1)} %copy-done.65), channel_id=1, source_target_pairs={{0,4},{1,3},{2,6},{3,1},{4,0},{5,7},{6,2},{7,5},{8,12},{9,11},{10,... | collective-permute-start | bytes 2211848 | tf_op jit(solution)/shard_map/ppermute | solution.py:263
  118.7 33.0 %collective-permute-start.20 = (bf16[2896,128]{1,0:T(8,128)(2,1)S(1)}, bf16[2896,128]{1,0:T(8,128)(2,1)S(1)}, u32[]{:S(2)}, u32[]{:S(2)}) collective-permute-start(bf16[2896,128]{1,0:T(8,128)(2,1)S(1)} %collective-permute-done.19.own_info.own_ref), channel_id=1, source_target_pairs={{0,2},{1,5},{2,0},{3,7},{4,6},{5,1},{6,4},{7,3},{8,10},{9,13},{10,... | collective-permute-start | bytes 2224136 | tf_op jit(solution)/shard_map/ppermute | solution.py:259
  161.3 15.5 %collective-permute-start.21 = (bf16[2,64,2880]{2,1,0:T(8,128)(2,1)}, bf16[2,64,2880]{2,1,0:T(8,128)(2,1)S(1)}, u32[]{:S(2)}, u32[]{:S(2)}) collective-permute-start(bf16[2,64,2880]{2,1,0:T(8,128)(2,1)} %get-tuple-element.96), channel_id=1, source_target_pairs={{0,4},{1,3},{2,6},{3,1},{4,0},{5,7},{6,2},{7,5},{8,12},{9,11},{10,... | collective-permute-start | bytes 2211848 | tf_op jit(solution)/shard_map/ppermute | solution.py:263
  162.5 15.6 %collective-permute-start.45 = (bf16[2,64,2880]{2,1,0:T(8,128)(2,1)S(1)}, bf16[2,64,2880]{2,1,0:T(8,128)(2,1)S(1)}, u32[]{:S(2)}, u32[]{:S(2)}) collective-permute-start(bf16[2,64,2880]{2,1,0:T(8,128)(2,1)S(1)} %copy-done.64), channel_id=1, source_target_pairs={{0,1},{1,0},{2,3},{3,2},{4,5},{5,4},{6,7},{7,6},{8,9},{9,8},{10,11... | collective-permute-start | bytes 2211848 | tf_op jit(solution)/shard_map/ppermute | solution.py:255
  162.7 22.2 %collective-permute-start.34 = (bf16[2,64,2880]{2,1,0:T(8,128)(2,1)S(1)}, bf16[2,64,2880]{2,1,0:T(8,128)(2,1)S(1)}, u32[]{:S(2)}, u32[]{:S(2)}) collective-permute-start(bf16[2,64,2880]{2,1,0:T(8,128)(2,1)S(1)} %pad_maximum_fusion.11), channel_id=1, source_target_pairs={{0,4},{1,3},{2,6},{3,1},{4,0},{5,7},{6,2},{7,5},{8,12},{9,11},{10,... | collective-permute-start | bytes 2211848 | tf_op jit(solution)/shard_map/ppermute | solution.py:263
  164.8 32.4 %collective-permute-start.26 = (bf16[2,64,2880]{2,1,0:T(8,128)(2,1)S(1)}, bf16[2,64,2880]{2,1,0:T(8,128)(2,1)}, u32[]{:S(2)}, u32[]{:S(2)}) collective-permute-start(bf16[2,64,2880]{2,1,0:T(8,128)(2,1)S(1)} %pad_maximum_fusion.7), channel_id=1, source_target_pairs={{0,1},{1,0},{2,3},{3,2},{4,5},{5,4},{6,7},{7,6},{8,9},{9,8},{10,11... | collective-permute-start | bytes 2211848 | tf_op jit(solution)/shard_map/ppermute | solution.py:255
  168.7 29.7 %collective-permute-start.18 = (bf16[2,64,2880]{2,1,0:T(8,128)(2,1)S(1)}, bf16[2,64,2880]{2,1,0:T(8,128)(2,1)}, u32[]{:S(2)}, u32[]{:S(2)}) collective-permute-start(bf16[2,64,2880]{2,1,0:T(8,128)(2,1)S(1)} %pad_maximum_fusion.5), channel_id=1, source_target_pairs={{0,1},{1,0},{2,3},{3,2},{4,5},{5,4},{6,7},{7,6},{8,9},{9,8},{10,11... | collective-permute-start | bytes 2211848 | tf_op jit(solution)/shard_map/ppermute | solution.py:255
  176.8 16.1 %collective-permute-start.49 = (bf16[2,64,2880]{2,1,0:T(8,128)(2,1)}, bf16[2,64,2880]{2,1,0:T(8,128)(2,1)S(1)}, u32[]{:S(2)}, u32[]{:S(2)}) collective-permute-start(bf16[2,64,2880]{2,1,0:T(8,128)(2,1)} %pad_maximum_fusion.15), channel_id=1, source_target_pairs={{0,4},{1,3},{2,6},{3,1},{4,0},{5,7},{6,2},{7,5},{8,12},{9,11},{10,... | collective-permute-start | bytes 2211848 | tf_op jit(solution)/shard_map/ppermute | solution.py:263
  178.1 20.3 %collective-permute-start.30 = (bf16[2,64,2880]{2,1,0:T(8,128)(2,1)S(1)}, bf16[2,64,2880]{2,1,0:T(8,128)(2,1)}, u32[]{:S(2)}, u32[]{:S(2)}) collective-permute-start(bf16[2,64,2880]{2,1,0:T(8,128)(2,1)S(1)} %pad_maximum_fusion.8), channel_id=1, source_target_pairs={{0,1},{1,0},{2,3},{3,2},{4,5},{5,4},{6,7},{7,6},{8,9},{9,8},{10,11... | collective-permute-start | bytes 2211848 | tf_op jit(solution)/shard_map/ppermute | solution.py:255
  192.9 37.0 %collective-permute-start.41 = (bf16[2880,128]{1,0:T(8,128)(2,1)}, bf16[2880,128]{1,0:T(8,128)(2,1)}, u32[]{:S(2)}, u32[]{:S(2)}) collective-permute-start(bf16[2880,128]{1,0:T(8,128)(2,1)} %get-tuple-element.123), channel_id=1, source_target_pairs={{0,2},{1,5},{2,0},{3,7},{4,6},{5,1},{6,4},{7,3},{8,10},{9,13},{10,... | collective-permute-start | bytes 2211848 | tf_op jit(solution)/shard_map/ppermute | solution.py:259
  197.2 35.8 %collective-permute-start.56 = (bf16[2880,128]{1,0:T(8,128)(2,1)}, bf16[2880,128]{1,0:T(8,128)(2,1)}, u32[]{:S(2)}, u32[]{:S(2)}) collective-permute-start(bf16[2880,128]{1,0:T(8,128)(2,1)} %get-tuple-element.146), channel_id=1, source_target_pairs={{0,2},{1,5},{2,0},{3,7},{4,6},{5,1},{6,4},{7,3},{8,10},{9,13},{10,... | collective-permute-start | bytes 2211848 | tf_op jit(solution)/shard_map/ppermute | solution.py:259
  229.8 21.9 %collective-permute-start.46 = (bf16[2,64,2880]{2,1,0:T(8,128)(2,1)}, bf16[2,64,2880]{2,1,0:T(8,128)(2,1)S(1)}, u32[]{:S(2)}, u32[]{:S(2)}) collective-permute-start(bf16[2,64,2880]{2,1,0:T(8,128)(2,1)} %get-tuple-element.128), channel_id=1, source_target_pairs={{0,1},{1,0},{2,3},{3,2},{4,5},{5,4},{6,7},{7,6},{8,9},{9,8},{10,11... | collective-permute-start | bytes 2211848 | tf_op jit(solution)/shard_map/ppermute | solution.py:255
  232.8 25.6 %collective-permute-start.42 = (bf16[2880,128]{1,0:T(8,128)(2,1)}, bf16[2880,128]{1,0:T(8,128)(2,1)}, u32[]{:S(2)}, u32[]{:S(2)}) collective-permute-start(bf16[2880,128]{1,0:T(8,128)(2,1)} %add_convert_fusion.7), channel_id=1, source_target_pairs={{0,8},{1,9},{2,10},{3,11},{4,12},{5,13},{6,14},{7,15},{8,16},{9,17... | collective-permute-start | bytes 2211848 | tf_op jit(solution)/shard_map/ppermute | solution.py:267
  236.4 43.7 %collective-permute-start.57 = (bf16[2880,128]{1,0:T(8,128)(2,1)}, bf16[2880,128]{1,0:T(8,128)(2,1)S(1)}, u32[]{:S(2)}, u32[]{:S(2)}) collective-permute-start(bf16[2880,128]{1,0:T(8,128)(2,1)} %add_convert_fusion.3), channel_id=1, source_target_pairs={{0,8},{1,9},{2,10},{3,11},{4,12},{5,13},{6,14},{7,15},{8,16},{9,17... | collective-permute-start | bytes 2211848 | tf_op jit(solution)/shard_map/ppermute | solution.py:267
  236.6 16.3 %collective-permute-start.50 = (bf16[2,64,2880]{2,1,0:T(8,128)(2,1)S(1)}, bf16[2,64,2880]{2,1,0:T(8,128)(2,1)S(1)}, u32[]{:S(2)}, u32[]{:S(2)}) collective-permute-start(bf16[2,64,2880]{2,1,0:T(8,128)(2,1)S(1)} %pad_maximum_fusion.14), channel_id=1, source_target_pairs={{0,4},{1,3},{2,6},{3,1},{4,0},{5,7},{6,2},{7,5},{8,12},{9,11},{10,... | collective-permute-start | bytes 2211848 | tf_op jit(solution)/shard_map/ppermute | solution.py:263
  250.7 19.7 %collective-permute-start.40 = (bf16[2880,128]{1,0:T(8,128)(2,1)}, bf16[2880,128]{1,0:T(8,128)(2,1)}, u32[]{:S(2)}, u32[]{:S(2)}) collective-permute-start(bf16[2880,128]{1,0:T(8,128)(2,1)} %get-tuple-element.120), channel_id=1, source_target_pairs={{0,2},{1,5},{2,0},{3,7},{4,6},{5,1},{6,4},{7,3},{8,10},{9,13},{10,... | collective-permute-start | bytes 2211848 | tf_op jit(solution)/shard_map/ppermute | solution.py:259
  251.8 21.1 %collective-permute-start.36 = (bf16[2,64,2880]{2,1,0:T(8,128)(2,1)S(1)}, bf16[2,64,2880]{2,1,0:T(8,128)(2,1)S(1)}, u32[]{:S(2)}, u32[]{:S(2)}) collective-permute-start(bf16[2,64,2880]{2,1,0:T(8,128)(2,1)S(1)} %pad_maximum_fusion.9), channel_id=1, source_target_pairs={{0,4},{1,3},{2,6},{3,1},{4,0},{5,7},{6,2},{7,5},{8,12},{9,11},{10,... | collective-permute-start | bytes 2211848 | tf_op jit(solution)/shard_map/ppermute | solution.py:263
  257.3 28.8 %collective-permute-start.55 = (bf16[2880,128]{1,0:T(8,128)(2,1)}, bf16[2880,128]{1,0:T(8,128)(2,1)S(1)}, u32[]{:S(2)}, u32[]{:S(2)}) collective-permute-start(bf16[2880,128]{1,0:T(8,128)(2,1)} %get-tuple-element.143), channel_id=1, source_target_pairs={{0,2},{1,5},{2,0},{3,7},{4,6},{5,1},{6,4},{7,3},{8,10},{9,13},{10,... | collective-permute-start | bytes 2211848 | tf_op jit(solution)/shard_map/ppermute | solution.py:259
  258.5 30.3 %collective-permute-start.51 = (bf16[2,64,2880]{2,1,0:T(8,128)(2,1)S(1)}, bf16[2,64,2880]{2,1,0:T(8,128)(2,1)S(1)}, u32[]{:S(2)}, u32[]{:S(2)}) collective-permute-start(bf16[2,64,2880]{2,1,0:T(8,128)(2,1)S(1)} %pad_maximum_fusion.13), channel_id=1, source_target_pairs={{0,4},{1,3},{2,6},{3,1},{4,0},{5,7},{6,2},{7,5},{8,12},{9,11},{10,... | collective-permute-start | bytes 2211848 | tf_op jit(solution)/shard_map/ppermute | solution.py:263
  272.8 21.4 %collective-permute-start.43 = (bf16[2880,128]{1,0:T(8,128)(2,1)}, bf16[2880,128]{1,0:T(8,128)(2,1)}, u32[]{:S(2)}, u32[]{:S(2)}) collective-permute-start(bf16[2880,128]{1,0:T(8,128)(2,1)} %add_convert_fusion.6), channel_id=1, source_target_pairs={{0,8},{1,9},{2,10},{3,11},{4,12},{5,13},{6,14},{7,15},{8,16},{9,17... | collective-permute-start | bytes 2211848 | tf_op jit(solution)/shard_map/ppermute | solution.py:267
  279.0 23.0 %collective-permute-start.39 = (bf16[2880,128]{1,0:T(8,128)(2,1)}, bf16[2880,128]{1,0:T(8,128)(2,1)}, u32[]{:S(2)}, u32[]{:S(2)}) collective-permute-start(bf16[2880,128]{1,0:T(8,128)(2,1)} %get-tuple-element.117), channel_id=1, source_target_pairs={{0,2},{1,5},{2,0},{3,7},{4,6},{5,1},{6,4},{7,3},{8,10},{9,13},{10,... | collective-permute-start | bytes 2211848 | tf_op jit(solution)/shard_map/ppermute | solution.py:259
  280.1 23.9 %collective-permute-start.37 = (bf16[2,64,2880]{2,1,0:T(8,128)(2,1)S(1)}, bf16[2,64,2880]{2,1,0:T(8,128)(2,1)S(1)}, u32[]{:S(2)}, u32[]{:S(2)}) collective-permute-start(bf16[2,64,2880]{2,1,0:T(8,128)(2,1)S(1)} %pad_maximum_fusion.4), channel_id=1, source_target_pairs={{0,4},{1,3},{2,6},{3,1},{4,0},{5,7},{6,2},{7,5},{8,12},{9,11},{10,... | collective-permute-start | bytes 2211848 | tf_op jit(solution)/shard_map/ppermute | solution.py:263
  288.3 23.5 %collective-permute-start.58 = (bf16[2880,128]{1,0:T(8,128)(2,1)S(1)}, bf16[2880,128]{1,0:T(8,128)(2,1)S(1)}, u32[]{:S(2)}, u32[]{:S(2)}) collective-permute-start(bf16[2880,128]{1,0:T(8,128)(2,1)S(1)} %add_convert_fusion.2), channel_id=1, source_target_pairs={{0,8},{1,9},{2,10},{3,11},{4,12},{5,13},{6,14},{7,15},{8,16},{9,17... | collective-permute-start | bytes 2211848 | tf_op jit(solution)/shard_map/ppermute | solution.py:267
  293.1 24.5 %collective-permute-start.54 = (bf16[2880,128]{1,0:T(8,128)(2,1)}, bf16[2880,128]{1,0:T(8,128)(2,1)S(1)}, u32[]{:S(2)}, u32[]{:S(2)}) collective-permute-start(bf16[2880,128]{1,0:T(8,128)(2,1)} %get-tuple-element.140), channel_id=1, source_target_pairs={{0,2},{1,5},{2,0},{3,7},{4,6},{5,1},{6,4},{7,3},{8,10},{9,13},{10,... | collective-permute-start | bytes 2211848 | tf_op jit(solution)/shard_map/ppermute | solution.py:259
  294.3 27.3 %collective-permute-start.52 = (bf16[2,64,2880]{2,1,0:T(8,128)(2,1)S(1)}, bf16[2,64,2880]{2,1,0:T(8,128)(2,1)S(1)}, u32[]{:S(2)}, u32[]{:S(2)}) collective-permute-start(bf16[2,64,2880]{2,1,0:T(8,128)(2,1)S(1)} %pad_maximum_fusion.12), channel_id=1, source_target_pairs={{0,4},{1,3},{2,6},{3,1},{4,0},{5,7},{6,2},{7,5},{8,12},{9,11},{10,... | collective-permute-start | bytes 2211848 | tf_op jit(solution)/shard_map/ppermute | solution.py:263
  303.5 27.3 %collective-permute-start.44 = (bf16[2880,128]{1,0:T(8,128)(2,1)S(1)}, bf16[2880,128]{1,0:T(8,128)(2,1)S(1)}, u32[]{:S(2)}, u32[]{:S(2)}) collective-permute-start(bf16[2880,128]{1,0:T(8,128)(2,1)S(1)} %add_convert_fusion.5), channel_id=1, source_target_pairs={{0,8},{1,9},{2,10},{3,11},{4,12},{5,13},{6,14},{7,15},{8,16},{9,17... | collective-permute-start | bytes 2211848 | tf_op jit(solution)/shard_map/ppermute | solution.py:267
  311.8 19.1 %collective-permute-start.38 = (bf16[2880,128]{1,0:T(8,128)(2,1)}, bf16[2880,128]{1,0:T(8,128)(2,1)S(1)}, u32[]{:S(2)}, u32[]{:S(2)}) collective-permute-start(bf16[2880,128]{1,0:T(8,128)(2,1)} %get-tuple-element.114), channel_id=1, source_target_pairs={{0,2},{1,5},{2,0},{3,7},{4,6},{5,1},{6,4},{7,3},{8,10},{9,13},{10,... | collective-permute-start | bytes 2211848 | tf_op jit(solution)/shard_map/ppermute | solution.py:259
  325.9 16.7 %collective-permute-start.59 = (bf16[2880,128]{1,0:T(8,128)(2,1)S(1)}, bf16[2880,128]{1,0:T(8,128)(2,1)S(1)}, u32[]{:S(2)}, u32[]{:S(2)}) collective-permute-start(bf16[2880,128]{1,0:T(8,128)(2,1)S(1)} %add_convert_fusion.1), channel_id=1, source_target_pairs={{0,8},{1,9},{2,10},{3,11},{4,12},{5,13},{6,14},{7,15},{8,16},{9,17... | collective-permute-start | bytes 2211848 | tf_op jit(solution)/shard_map/ppermute | solution.py:267
  (84 other events, 660.6 us)

commit v3 on v2

--- a/solution.py
+++ b/solution.py
@@ -392,12 +392,12 @@
             total = value.astype(BF16)
         return total, routes
 
+    d_tokens, _ = gather(grads, 0)
     output, routes = gather(parts, 1)
     route = jnp.stack([r[0][0] for r in routes]) + with_near(jnp.stack([r[0][1] for r in routes]))
     d_route = route[0]
     for step in (1, 2, 3):
         d_route = d_route + to_next_plane(route[step], -step)
-    d_tokens, _ = gather(grads, 0)
     return (output.T, d_tokens.T, d_route.T)
 
 

time: 351 us -> 351 us (level)
  no operation moved by 1% of the time
where the time goes in v3:
time: 351 us; the launch traced here: 344 us
  waiting for transfers between devices  125 us (36%)
  Pallas kernels  123 us (35%)
  starting transfers between devices  57.5 us (16%)
  other arithmetic  20.7 us (6%)
  local copies, waits for them, and re-layouts  15.9 us (5%)
    pallas_call x2, Pallas kernels, run_experts(): pl.pallas_call(functools.partial(experts_kernel, experts, planes), out_sh...  61.5 us
    ppermute x15, waiting for transfers between devices, to_next_plane(): lax.ppermute(value, AXES, [(n, (n + 8 * by) % 32) for n in range(32)])  54.3 us
    ppermute x16, waiting for transfers between devices, with_far(): lax.ppermute(value, AXES, [(n, n ^ (COL if n & CORE else ROW)) for n in r...  40.7 us
    pallas_call x8, Pallas kernels, gather(): pl.pallas_call(functools.partial(combine_out_kernel if outputs else combi...  33.9 us
    ppermute x17, waiting for transfers between devices, with_near(): lax.ppermute(value, AXES, [(n, n ^ (ROW if n & CORE else COL)) for n in r...  29.9 us
    pallas_call x8, Pallas kernels, spread(): pl.pallas_call(functools.partial(pack_kernel, slots, experts, scaled), ou...  27.6 us
    ppermute x17, starting transfers between devices, with_near(): lax.ppermute(value, AXES, [(n, n ^ (ROW if n & CORE else COL)) for n in r...  19.2 us
    ppermute x16, starting transfers between devices, with_far(): lax.ppermute(value, AXES, [(n, n ^ (COL if n & CORE else ROW)) for n in r...  16.4 us
  transfers between devices with their start and end apart: 64, of which 19 were waited for; matrix products, arithmetic and copies ran while one was open for 7% of the time, Pallas kernels for 36%

profile of v3, /device:TPU:0, one launch (start us, length us, event | category | flops | bytes accessed | tf_op | source)
XLA Modules:
  0.0 344.3 jit_solution(16242595415744958595)
XLA Ops:
  0.6 3.1 collective-permute-start.10
  6.0 2.9 concatenate.6.own_info.own_ref
  8.9 1.6 collective-permute-start.3
  12.6 10.8 %collective-permute-done.10.own_ref.d_own_ref = bf16[2880,128]{1,0:T(8,128)(2,1)} collective-permute-done((bf16[2880,128]{1,0:T(8,128)(2,1)}, bf16[2880,128]{1,0:T(8,128)(2,1)}, u32[]{:S(2)}, u32[]{:S(2)}) %collective-permute-start.10) | collective-permute-done | bytes 737312 | tf_op jit(solution)/shard_map/ppermute | solution.py:267
  23.4 1.7 collective-permute-start.11
  25.1 13.2 %collective-permute-done.3.own_info.own_ref = bf16[2896,128]{1,0:T(8,128)(2,1)S(1)} collective-permute-done((bf16[2896,128]{1,0:T(8,128)(2,1)S(1)}, bf16[2896,128]{1,0:T(8,128)(2,1)S(1)}, u32[]{:S(2)}, u32[]{:S(2)}) %collective-permute-start.3) | collective-permute-done | bytes 741408 | tf_op jit(solution)/shard_map/ppermute | solution.py:267
  41.4 3.4 pack_gradients.4
  47.6 3.4 pack_tokens.4
  51.5 1.7 collective-permute-done.4.other_info.other_ref
  54.1 3.5 %pack_gradients.5 = (bf16[64,2880]{1,0:T(8,128)(2,1)}, bf16[64,2880]{1,0:T(8,128)(2,1)}, bf16[2,64,2880]{2,1,0:T(8,128)(2,1)}) custom-call(s32[2]{0:T(128)} %pad_add_fusion.pos_ref, bf16[2896,128]{1,0:T(8,128)(2,1)} %copy-done.6, bf16[2896,128]{1,0:T(8,128)(2,1)} %copy-done.7, bf16[2880,128]{1,0:T(8,128)(2,1)} %collective-permute-done.10.own_ref.d_own_ref, ...), custom_call_target="tpu_custom_call" | custom-call | flops 377487360 | bytes 2211840 | tf_op jit(solution)/shard_map/pack_gradients/pallas_call | solution.py:309
  57.6 2.3 collective-permute-start.12
  59.9 3.5 %pack_tokens.5 = (bf16[64,2880]{1,0:T(8,128)(2,1)}, bf16[64,2880]{1,0:T(8,128)(2,1)}, bf16[2,64,2880]{2,1,0:T(8,128)(2,1)}) custom-call(s32[2]{0:T(128)} %pad_add_fusion.pos_ref, bf16[2896,128]{1,0:T(8,128)(2,1)} %copy-done.6, bf16[2896,128]{1,0:T(8,128)(2,1)} %copy-done.7, bf16[2896,128]{1,0:T(8,128)(2,1)} %copy-done.6, bf16[2896,128]{1,0:T(8,128)(2,1)} %copy-done.7), custom_call_target="tpu_custom_call" | custom-call | flops 377487360 | bytes 2211840 | tf_op jit(solution)/shard_map/pack_tokens/pallas_call | solution.py:309
  64.7 1.7 collective-permute-start.24
  66.4 11.4 %collective-permute-done.15.own_info.own_ref = bf16[2896,128]{1,0:T(8,128)(2,1)S(1)} collective-permute-done((bf16[2896,128]{1,0:T(8,128)(2,1)S(1)}, bf16[2896,128]{1,0:T(8,128)(2,1)S(1)}, u32[]{:S(2)}, u32[]{:S(2)}) %collective-permute-start.15) | collective-permute-done | bytes 741408 | tf_op jit(solution)/shard_map/ppermute | solution.py:267
  78.4 1.6 collective-permute-start.9
  80.1 12.9 %collective-permute-done.5.refs_4_ = bf16[2,64,2880]{2,1,0:T(8,128)(2,1)S(1)} collective-permute-done((bf16[2,64,2880]{2,1,0:T(8,128)(2,1)}, bf16[2,64,2880]{2,1,0:T(8,128)(2,1)S(1)}, u32[]{:S(2)}, u32[]{:S(2)}) %collective-permute-start.5) | collective-permute-done | bytes 737312 | tf_op jit(solution)/shard_map/ppermute | solution.py:263
  92.9 3.1 collective-permute-start.2
  100.0 3.5 %pack_tokens.6 = (bf16[64,2880]{1,0:T(8,128)(2,1)}, bf16[64,2880]{1,0:T(8,128)(2,1)}, bf16[2,64,2880]{2,1,0:T(8,128)(2,1)}) custom-call(s32[2]{0:T(128)} %pad_add_fusion.pos_ref, bf16[2896,128]{1,0:T(8,128)(2,1)} %copy-done.2, bf16[2896,128]{1,0:T(8,128)(2,1)} %copy-done.4, bf16[2896,128]{1,0:T(8,128)(2,1)} %copy-done.2, bf16[2896,128]{1,0:T(8,128)(2,1)} %copy-done.4), custom_call_target="tpu_custom_call" | custom-call | flops 377487360 | bytes 2211840 | tf_op jit(solution)/shard_map/pack_tokens/pallas_call | solution.py:309
  103.4 3.5 %pack_gradients.6 = (bf16[64,2880]{1,0:T(8,128)(2,1)}, bf16[64,2880]{1,0:T(8,128)(2,1)}, bf16[2,64,2880]{2,1,0:T(8,128)(2,1)}) custom-call(s32[2]{0:T(128)} %pad_add_fusion.pos_ref, bf16[2896,128]{1,0:T(8,128)(2,1)} %copy-done.2, bf16[2896,128]{1,0:T(8,128)(2,1)} %copy-done.4, bf16[2880,128]{1,0:T(8,128)(2,1)} %copy-done.8, bf16[2880,128]{1,0:T(8,128)(2,1)} %copy-done.9), custom_call_target="tpu_custom_call" | custom-call | flops 377487360 | bytes 2211840 | tf_op jit(solution)/shard_map/pack_gradients/pallas_call | solution.py:309
  109.3 8.2 %collective-permute-done.19.own_info.own_ref = bf16[2896,128]{1,0:T(8,128)(2,1)S(1)} collective-permute-done((bf16[2896,128]{1,0:T(8,128)(2,1)S(1)}, bf16[2896,128]{1,0:T(8,128)(2,1)S(1)}, u32[]{:S(2)}, u32[]{:S(2)}) %collective-permute-start.19) | collective-permute-done | bytes 741408 | tf_op jit(solution)/shard_map/ppermute | solution.py:267
  119.9 30.7 %experts.2 = (bf16[64,2880]{1,0:T(8,128)(2,1)}, bf16[64,2880]{1,0:T(8,128)(2,1)}, bf16[2,64,2880]{2,1,0:T(8,128)(2,1)}, bf16[64,2880]{1,0:T(8,128)(2,1)}, bf16[6...) custom-call(s32[2]{0:T(128)} %pad_add_fusion.pos_ref, ...), custom_call_target="tpu_custom_call" | custom-call | flops 12740198400 | bytes 49766400 | tf_op jit(solution)/shard_map/experts/pallas_call | solution.py:339
  153.4 3.4 pack_gradients.7
  157.9 3.4 pack_tokens.7
  164.8 3.9 %collective-permute-done.29.refs_10_ = bf16[2,64,2880]{2,1,0:T(8,128)(2,1)S(1)} collective-permute-done((bf16[2,64,2880]{2,1,0:T(8,128)(2,1)}, bf16[2,64,2880]{2,1,0:T(8,128)(2,1)S(1)}, u32[]{:S(2)}, u32[]{:S(2)}) %collective-permute-start.29) | collective-permute-done | bytes 737312 | tf_op jit(solution)/shard_map/ppermute | solution.py:263
  168.7 8.0 %collective-permute-done.21.refs_4_ = bf16[2,64,2880]{2,1,0:T(8,128)(2,1)S(1)} collective-permute-done((bf16[2,64,2880]{2,1,0:T(8,128)(2,1)}, bf16[2,64,2880]{2,1,0:T(8,128)(2,1)S(1)}, u32[]{:S(2)}, u32[]{:S(2)}) %collective-permute-start.21) | collective-permute-done | bytes 737312 | tf_op jit(solution)/shard_map/ppermute | solution.py:263
  178.2 6.7 %collective-permute-done.34.far_ref = bf16[2,64,2880]{2,1,0:T(8,128)(2,1)S(1)} collective-permute-done((bf16[2,64,2880]{2,1,0:T(8,128)(2,1)S(1)}, bf16[2,64,2880]{2,1,0:T(8,128)(2,1)S(1)}, u32[]{:S(2)}, u32[]{:S(2)}) %collective-permute-start.34) | collective-permute-done | bytes 737312 | tf_op jit(solution)/shard_map/ppermute | solution.py:263
  186.0 5.0 %sum_outputs.7 = (f32[2880,128]{1,0:T(8,128)}, bf16[2880,128]{1,0:T(8,128)(2,1)}, f32[2,2,128]{2,1,0:T(2,128)}) custom-call(s32[2]{0:T(128)} %pad_add_fusion.pos_ref, bf16[2896,128]{1,0:T(8,128)(2,1)} %copy-done.6, bf16[2896,128]{1,0:T(8,128)(2,1)} %copy-done.7, bf16[64,2880]{1,0:T(8,128)(2,1)} %get-tuple-element.121.kept_ref, ...), custom_call_target="tpu_custom_call" | custom-call | flops 377487360 | bytes 2211840 | tf_op jit(solution)/shard_map/sum_outputs/pallas_call | solution.py:374
  191.0 2.0 collective-permute-done.49.far_ref
  193.8 3.3 sum_gradients.7
  198.4 30.8 %experts.3 = (bf16[64,2880]{1,0:T(8,128)(2,1)}, bf16[64,2880]{1,0:T(8,128)(2,1)}, bf16[2,64,2880]{2,1,0:T(8,128)(2,1)}, bf16[64,2880]{1,0:T(8,128)(2,1)}, bf16[6...) custom-call(s32[2]{0:T(128)} %pad_add_fusion.pos_ref, ...), custom_call_target="tpu_custom_call" | custom-call | flops 12740198400 | bytes 49766400 | tf_op jit(solution)/shard_map/experts/pallas_call | solution.py:339
  230.3 2.2 add_convert_fusion.7
  234.2 2.3 add_convert_fusion.3
  237.8 6.9 %collective-permute-done.35.far_ref = bf16[2,64,2880]{2,1,0:T(8,128)(2,1)S(1)} collective-permute-done((bf16[2,64,2880]{2,1,0:T(8,128)(2,1)S(1)}, bf16[2,64,2880]{2,1,0:T(8,128)(2,1)S(1)}, u32[]{:S(2)}, u32[]{:S(2)}) %collective-permute-start.35) | collective-permute-done | bytes 737312 | tf_op jit(solution)/shard_map/ppermute | solution.py:263
  245.6 5.1 %sum_outputs.6 = (f32[2880,128]{1,0:T(8,128)}, bf16[2880,128]{1,0:T(8,128)(2,1)}, f32[2,2,128]{2,1,0:T(2,128)}) custom-call(s32[2]{0:T(128)} %pad_add_fusion.pos_ref, bf16[2896,128]{1,0:T(8,128)(2,1)} %copy-done.2, bf16[2896,128]{1,0:T(8,128)(2,1)} %copy-done.4, bf16[64,2880]{1,0:T(8,128)(2,1)} %get-tuple-element.118.kept_ref, ...), custom_call_target="tpu_custom_call" | custom-call | flops 377487360 | bytes 2211840 | tf_op jit(solution)/shard_map/sum_outputs/pallas_call | solution.py:374
  253.8 3.5 %sum_gradients.6 = (f32[2880,128]{1,0:T(8,128)}, bf16[2880,128]{1,0:T(8,128)(2,1)}) custom-call(s32[2]{0:T(128)} %pad_add_fusion.pos_ref, bf16[2896,128]{1,0:T(8,128)(2,1)} %copy-done.2, bf16[2896,128]{1,0:T(8,128)(2,1)} %copy-done.4, bf16[64,2880]{1,0:T(8,128)(2,1)} %get-tuple-element.141.kept_ref, bf16[2,64,2880]{2,1,0:T(8,128)(2,1)} %copy-done.17, ...), custom_call_target="tpu_custom_call" | custom-call | flops 377487360 | bytes 2211840 | tf_op jit(solution)/shard_map/sum_gradients/pallas_call | solution.py:374
  259.5 10.8 %collective-permute-done.40 = bf16[2880,128]{1,0:T(8,128)(2,1)} collective-permute-done((bf16[2880,128]{1,0:T(8,128)(2,1)}, bf16[2880,128]{1,0:T(8,128)(2,1)}, u32[]{:S(2)}, u32[]{:S(2)}) %collective-permute-start.40) | collective-permute-done | bytes 737312 | tf_op jit(solution)/shard_map/ppermute | solution.py:259
  270.4 2.4 add_convert_fusion.6
  273.9 5.1 %sum_outputs.5 = (f32[2880,128]{1,0:T(8,128)}, bf16[2880,128]{1,0:T(8,128)(2,1)}, f32[2,2,128]{2,1,0:T(2,128)}) custom-call(s32[2]{0:T(128)} %pad_add_fusion.pos_ref, bf16[2896,128]{1,0:T(8,128)(2,1)} %copy-done.3, bf16[2896,128]{1,0:T(8,128)(2,1)} %copy-done.5, bf16[64,2880]{1,0:T(8,128)(2,1)} %get-tuple-element.115.kept_ref, ...), custom_call_target="tpu_custom_call" | custom-call | flops 377487360 | bytes 2211840 | tf_op jit(solution)/shard_map/sum_outputs/pallas_call | solution.py:374
  280.7 5.3 %collective-permute-done.55 = bf16[2880,128]{1,0:T(8,128)(2,1)S(1)} collective-permute-done((bf16[2880,128]{1,0:T(8,128)(2,1)}, bf16[2880,128]{1,0:T(8,128)(2,1)S(1)}, u32[]{:S(2)}, u32[]{:S(2)}) %collective-permute-start.55) | collective-permute-done | bytes 737312 | tf_op jit(solution)/shard_map/ppermute | solution.py:259
  289.6 3.5 %sum_gradients.5 = (f32[2880,128]{1,0:T(8,128)}, bf16[2880,128]{1,0:T(8,128)(2,1)}) custom-call(s32[2]{0:T(128)} %pad_add_fusion.pos_ref, bf16[2896,128]{1,0:T(8,128)(2,1)} %copy-done.3, bf16[2896,128]{1,0:T(8,128)(2,1)} %copy-done.5, bf16[64,2880]{1,0:T(8,128)(2,1)} %get-tuple-element.138.kept_ref, bf16[2,64,2880]{2,1,0:T(8,128)(2,1)} %copy-done.13, ...), custom_call_target="tpu_custom_call" | custom-call | flops 377487360 | bytes 2211840 | tf_op jit(solution)/shard_map/sum_gradients/pallas_call | solution.py:374
  294.9 7.0 %collective-permute-done.39 = bf16[2880,128]{1,0:T(8,128)(2,1)} collective-permute-done((bf16[2880,128]{1,0:T(8,128)(2,1)}, bf16[2880,128]{1,0:T(8,128)(2,1)}, u32[]{:S(2)}, u32[]{:S(2)}) %collective-permute-start.39) | collective-permute-done | bytes 737312 | tf_op jit(solution)/shard_map/ppermute | solution.py:259
  302.0 1.6 add_convert_fusion.5
  304.9 5.1 %sum_outputs.4 = (f32[2880,128]{1,0:T(8,128)}, bf16[2880,128]{1,0:T(8,128)(2,1)}, f32[2,2,128]{2,1,0:T(2,128)}) custom-call(s32[2]{0:T(128)} %pad_add_fusion.pos_ref, bf16[2896,128]{1,0:T(8,128)(2,1)} %copy-done, bf16[2896,128]{1,0:T(8,128)(2,1)} %copy-done.1, bf16[64,2880]{1,0:T(8,128)(2,1)} %get-tuple-element.89.kept_ref, bf16[2,64,2880]{2,1,0:T(8,128)(2,1)} %copy-done.12, ...), custom_call_target="tpu_custom_call" | custom-call | flops 377487360 | bytes 2211840 | tf_op jit(solution)/shard_map/sum_outputs/pallas_call | solution.py:374
  312.7 5.0 %collective-permute-done.54 = bf16[2880,128]{1,0:T(8,128)(2,1)S(1)} collective-permute-done((bf16[2880,128]{1,0:T(8,128)(2,1)}, bf16[2880,128]{1,0:T(8,128)(2,1)S(1)}, u32[]{:S(2)}, u32[]{:S(2)}) %collective-permute-start.54) | collective-permute-done | bytes 737312 | tf_op jit(solution)/shard_map/ppermute | solution.py:259
  317.9 3.6 %collective-permute-start.61 = (f32[2,128]{1,0:T(2,128)S(1)}, f32[2,128]{1,0:T(2,128)S(1)}, u32[]{:S(2)}, u32[]{:S(2)}) collective-permute-start(f32[2,128]{1,0:T(2,128)S(1)} %get-tuple-element.151), channel_id=1, source_target_pairs={{0,24},{1,25},{2,26},{3,27},{4,28},{5,29},{6,30},{7,31},{8,0},{9,1... | collective-permute-start | bytes 3080 | tf_op jit(solution)/shard_map/ppermute | solution.py:267
  322.5 3.5 %sum_gradients.4 = (f32[2880,128]{1,0:T(8,128)}, bf16[2880,128]{1,0:T(8,128)(2,1)}) custom-call(s32[2]{0:T(128)} %pad_add_fusion.pos_ref, bf16[2896,128]{1,0:T(8,128)(2,1)} %copy-done, bf16[2896,128]{1,0:T(8,128)(2,1)} %copy-done.1, bf16[64,2880]{1,0:T(8,128)(2,1)} %get-tuple-element.124.kept_ref, bf16[2,64,2880]{2,1,0:T(8,128)(2,1)} %copy-done.11, ...), custom_call_target="tpu_custom_call" | custom-call | flops 377487360 | bytes 2211840 | tf_op jit(solution)/shard_map/sum_gradients/pallas_call | solution.py:374
  325.9 3.5 %collective-permute-start.59 = (bf16[2880,128]{1,0:T(8,128)(2,1)S(1)}, bf16[2880,128]{1,0:T(8,128)(2,1)S(1)}, u32[]{:S(2)}, u32[]{:S(2)}) collective-permute-start(bf16[2880,128]{1,0:T(8,128)(2,1)S(1)} %add_convert_fusion.1), channel_id=1, source_target_pairs={{0,8},{1,9},{2,10},{3,11},{4,12},{5,13},{6,14},{7,15},{8,16},{9,17... | collective-permute-start | bytes 2211848 | tf_op jit(solution)/shard_map/ppermute | solution.py:267
  332.0 10.6 %collective-permute-done.59 = bf16[2880,128]{1,0:T(8,128)(2,1)S(1)} collective-permute-done((bf16[2880,128]{1,0:T(8,128)(2,1)S(1)}, bf16[2880,128]{1,0:T(8,128)(2,1)S(1)}, u32[]{:S(2)}, u32[]{:S(2)}) %collective-permute-start.59) | collective-permute-done | bytes 737312 | tf_op jit(solution)/shard_map/ppermute | solution.py:267
  (289 shorter events, 61.2 us)
Async XLA Ops:
  0.6 22.7 %collective-permute-start.10 = (bf16[2880,128]{1,0:T(8,128)(2,1)}, bf16[2880,128]{1,0:T(8,128)(2,1)}, u32[]{:S(2)}, u32[]{:S(2)}) collective-permute-start(bf16[2880,128]{1,0:T(8,128)(2,1)} %bitcast.7.own_ref.d_own_ref), channel_id=1, source_target_pairs={{0,8},{1,9},{2,10},{3,11},{4,12},{5,13},{6,14},{7,15},{8,16},{9,17... | collective-permute-start | bytes 2211848 | tf_op jit(solution)/shard_map/ppermute | solution.py:267
  8.9 29.4 %collective-permute-start.3 = (bf16[2896,128]{1,0:T(8,128)(2,1)S(1)}, bf16[2896,128]{1,0:T(8,128)(2,1)S(1)}, u32[]{:S(2)}, u32[]{:S(2)}) collective-permute-start(bf16[2896,128]{1,0:T(8,128)(2,1)S(1)} %concatenate.6.own_info.own_ref), channel_id=1, source_target_pairs={{0,8},{1,9},{2,10},{3,11},{4,12},{5,13},{6,14},{7,15},{8,16},{9,17... | collective-permute-start | bytes 2224136 | tf_op jit(solution)/shard_map/ppermute | solution.py:267
  10.5 29.9 %collective-permute-start = (bf16[2896,128]{1,0:T(8,128)(2,1)S(1)}, bf16[2896,128]{1,0:T(8,128)(2,1)S(1)}, u32[]{:S(2)}, u32[]{:S(2)}) collective-permute-start(bf16[2896,128]{1,0:T(8,128)(2,1)S(1)} %concatenate.6.own_info.own_ref), channel_id=1, source_target_pairs={{0,2},{1,5},{2,0},{3,7},{4,6},{5,1},{6,4},{7,3},{8,10},{9,13},{10,... | collective-permute-start | bytes 2224136 | tf_op jit(solution)/shard_map/ppermute | solution.py:259
  12.0 28.4 %collective-permute-start.7 = (bf16[2880,128]{1,0:T(8,128)(2,1)}, bf16[2880,128]{1,0:T(8,128)(2,1)}, u32[]{:S(2)}, u32[]{:S(2)}) collective-permute-start(bf16[2880,128]{1,0:T(8,128)(2,1)} %bitcast.7.own_ref.d_own_ref), channel_id=1, source_target_pairs={{0,2},{1,5},{2,0},{3,7},{4,6},{5,1},{6,4},{7,3},{8,10},{9,13},{10,... | collective-permute-start | bytes 2211848 | tf_op jit(solution)/shard_map/ppermute | solution.py:259
  23.4 27.6 %collective-permute-start.11 = (bf16[2880,128]{1,0:T(8,128)(2,1)}, bf16[2880,128]{1,0:T(8,128)(2,1)}, u32[]{:S(2)}, u32[]{:S(2)}) collective-permute-start(bf16[2880,128]{1,0:T(8,128)(2,1)} %collective-permute-done.10.own_ref.d_own_ref), channel_id=1, source_target_pairs={{0,2},{1,5},{2,0},{3,7},{4,6},{5,1},{6,4},{7,3},{8,10},{9,13},{10,... | collective-permute-start | bytes 2211848 | tf_op jit(solution)/shard_map/ppermute | solution.py:259
  40.5 22.9 %collective-permute-start.23 = (bf16[2880,128]{1,0:T(8,128)(2,1)}, bf16[2880,128]{1,0:T(8,128)(2,1)S(1)}, u32[]{:S(2)}, u32[]{:S(2)}) collective-permute-start(bf16[2880,128]{1,0:T(8,128)(2,1)} %collective-permute-done.10.own_ref.d_own_ref), channel_id=1, source_target_pairs={{0,8},{1,9},{2,10},{3,11},{4,12},{5,13},{6,14},{7,15},{8,16},{9,17... | collective-permute-start | bytes 2211848 | tf_op jit(solution)/shard_map/ppermute | solution.py:267
  44.8 18.7 %collective-permute-start.8 = (bf16[2,64,2880]{2,1,0:T(8,128)(2,1)}, bf16[2,64,2880]{2,1,0:T(8,128)(2,1)S(1)}, u32[]{:S(2)}, u32[]{:S(2)}) collective-permute-start(bf16[2,64,2880]{2,1,0:T(8,128)(2,1)} %get-tuple-element.84), channel_id=1, source_target_pairs={{0,4},{1,3},{2,6},{3,1},{4,0},{5,7},{6,2},{7,5},{8,12},{9,11},{10,... | collective-permute-start | bytes 2211848 | tf_op jit(solution)/shard_map/ppermute | solution.py:263
  46.3 31.5 %collective-permute-start.15 = (bf16[2896,128]{1,0:T(8,128)(2,1)S(1)}, bf16[2896,128]{1,0:T(8,128)(2,1)S(1)}, u32[]{:S(2)}, u32[]{:S(2)}) collective-permute-start(bf16[2896,128]{1,0:T(8,128)(2,1)S(1)} %collective-permute-done.3.own_info.own_ref), channel_id=1, source_target_pairs={{0,8},{1,9},{2,10},{3,11},{4,12},{5,13},{6,14},{7,15},{8,16},{9,17... | collective-permute-start | bytes 2224136 | tf_op jit(solution)/shard_map/ppermute | solution.py:267
  57.6 20.8 %collective-permute-start.12 = (bf16[2,64,2880]{2,1,0:T(8,128)(2,1)}, bf16[2,64,2880]{2,1,0:T(8,128)(2,1)S(1)}, u32[]{:S(2)}, u32[]{:S(2)}) collective-permute-start(bf16[2,64,2880]{2,1,0:T(8,128)(2,1)} %get-tuple-element.87), channel_id=1, source_target_pairs={{0,4},{1,3},{2,6},{3,1},{4,0},{5,7},{6,2},{7,5},{8,12},{9,11},{10,... | collective-permute-start | bytes 2211848 | tf_op jit(solution)/shard_map/ppermute | solution.py:263
  63.4 29.6 %collective-permute-start.5 = (bf16[2,64,2880]{2,1,0:T(8,128)(2,1)}, bf16[2,64,2880]{2,1,0:T(8,128)(2,1)S(1)}, u32[]{:S(2)}, u32[]{:S(2)}) collective-permute-start(bf16[2,64,2880]{2,1,0:T(8,128)(2,1)} %get-tuple-element.81), channel_id=1, source_target_pairs={{0,4},{1,3},{2,6},{3,1},{4,0},{5,7},{6,2},{7,5},{8,12},{9,11},{10,... | collective-permute-start | bytes 2211848 | tf_op jit(solution)/shard_map/ppermute | solution.py:263
  63.5 33.6 %collective-permute-start.27 = (bf16[2880,128]{1,0:T(8,128)(2,1)S(1)}, bf16[2880,128]{1,0:T(8,128)(2,1)}, u32[]{:S(2)}, u32[]{:S(2)}) collective-permute-start(bf16[2880,128]{1,0:T(8,128)(2,1)S(1)} %collective-permute-done.23.own_ref.d_own_ref), channel_id=1, source_target_pairs={{0,8},{1,9},{2,10},{3,11},{4,12},{5,13},{6,14},{7,15},{8,16},{9,17... | collective-permute-start | bytes 2211848 | tf_op jit(solution)/shard_map/ppermute | solution.py:267
  64.7 33.4 %collective-permute-start.24 = (bf16[2880,128]{1,0:T(8,128)(2,1)S(1)}, bf16[2880,128]{1,0:T(8,128)(2,1)S(1)}, u32[]{:S(2)}, u32[]{:S(2)}) collective-permute-start(bf16[2880,128]{1,0:T(8,128)(2,1)S(1)} %collective-permute-done.23.own_ref.d_own_ref), channel_id=1, source_target_pairs={{0,2},{1,5},{2,0},{3,7},{4,6},{5,1},{6,4},{7,3},{8,10},{9,13},{10,... | collective-permute-start | bytes 2211848 | tf_op jit(solution)/shard_map/ppermute | solution.py:259
  77.8 20.5 %collective-permute-start.16 = (bf16[2896,128]{1,0:T(8,128)(2,1)S(1)}, bf16[2896,128]{1,0:T(8,128)(2,1)S(1)}, u32[]{:S(2)}, u32[]{:S(2)}) collective-permute-start(bf16[2896,128]{1,0:T(8,128)(2,1)S(1)} %collective-permute-done.15.own_info.own_ref), channel_id=1, source_target_pairs={{0,2},{1,5},{2,0},{3,7},{4,6},{5,1},{6,4},{7,3},{8,10},{9,13},{10,... | collective-permute-start | bytes 2224136 | tf_op jit(solution)/shard_map/ppermute | solution.py:259
  78.4 28.5 %collective-permute-start.9 = (bf16[2,64,2880]{2,1,0:T(8,128)(2,1)}, bf16[2,64,2880]{2,1,0:T(8,128)(2,1)}, u32[]{:S(2)}, u32[]{:S(2)}) collective-permute-start(bf16[2,64,2880]{2,1,0:T(8,128)(2,1)} %pad_maximum_fusion.2), channel_id=1, source_target_pairs={{0,1},{1,0},{2,3},{3,2},{4,5},{5,4},{6,7},{7,6},{8,9},{9,8},{10,11... | collective-permute-start | bytes 2211848 | tf_op jit(solution)/shard_map/ppermute | solution.py:255
  92.9 15.4 %collective-permute-start.2 = (bf16[2,64,2880]{2,1,0:T(8,128)(2,1)S(1)}, bf16[2,64,2880]{2,1,0:T(8,128)(2,1)}, u32[]{:S(2)}, u32[]{:S(2)}) collective-permute-start(bf16[2,64,2880]{2,1,0:T(8,128)(2,1)S(1)} %pad_maximum_fusion), channel_id=1, source_target_pairs={{0,1},{1,0},{2,3},{3,2},{4,5},{5,4},{6,7},{7,6},{8,9},{9,8},{10,11... | collective-permute-start | bytes 2211848 | tf_op jit(solution)/shard_map/ppermute | solution.py:255
  97.1 20.4 %collective-permute-start.19 = (bf16[2896,128]{1,0:T(8,128)(2,1)S(1)}, bf16[2896,128]{1,0:T(8,128)(2,1)S(1)}, u32[]{:S(2)}, u32[]{:S(2)}) collective-permute-start(bf16[2896,128]{1,0:T(8,128)(2,1)S(1)} %collective-permute-done.15.own_info.own_ref), channel_id=1, source_target_pairs={{0,8},{1,9},{2,10},{3,11},{4,12},{5,13},{6,14},{7,15},{8,16},{9,17... | collective-permute-start | bytes 2224136 | tf_op jit(solution)/shard_map/ppermute | solution.py:267
  98.1 20.5 %collective-permute-start.13 = (bf16[2,64,2880]{2,1,0:T(8,128)(2,1)}, bf16[2,64,2880]{2,1,0:T(8,128)(2,1)}, u32[]{:S(2)}, u32[]{:S(2)}) collective-permute-start(bf16[2,64,2880]{2,1,0:T(8,128)(2,1)} %pad_maximum_fusion.3), channel_id=1, source_target_pairs={{0,1},{1,0},{2,3},{3,2},{4,5},{5,4},{6,7},{7,6},{8,9},{9,8},{10,11... | collective-permute-start | bytes 2211848 | tf_op jit(solution)/shard_map/ppermute | solution.py:255
  99.1 20.8 %collective-permute-start.6 = (bf16[2,64,2880]{2,1,0:T(8,128)(2,1)}, bf16[2,64,2880]{2,1,0:T(8,128)(2,1)}, u32[]{:S(2)}, u32[]{:S(2)}) collective-permute-start(bf16[2,64,2880]{2,1,0:T(8,128)(2,1)} %pad_maximum_fusion.1), channel_id=1, source_target_pairs={{0,1},{1,0},{2,3},{3,2},{4,5},{5,4},{6,7},{7,6},{8,9},{9,8},{10,11... | collective-permute-start | bytes 2211848 | tf_op jit(solution)/shard_map/ppermute | solution.py:255
  106.9 44.7 %collective-permute-start.28 = (bf16[2880,128]{1,0:T(8,128)(2,1)}, bf16[2880,128]{1,0:T(8,128)(2,1)S(1)}, u32[]{:S(2)}, u32[]{:S(2)}) collective-permute-start(bf16[2880,128]{1,0:T(8,128)(2,1)} %collective-permute-done.27.own_ref.d_own_ref), channel_id=1, source_target_pairs={{0,2},{1,5},{2,0},{3,7},{4,6},{5,1},{6,4},{7,3},{8,10},{9,13},{10,... | collective-permute-start | bytes 2211848 | tf_op jit(solution)/shard_map/ppermute | solution.py:259
  108.3 42.4 %collective-permute-start.25 = (bf16[2,64,2880]{2,1,0:T(8,128)(2,1)}, bf16[2,64,2880]{2,1,0:T(8,128)(2,1)S(1)}, u32[]{:S(2)}, u32[]{:S(2)}) collective-permute-start(bf16[2,64,2880]{2,1,0:T(8,128)(2,1)} %get-tuple-element.99), channel_id=1, source_target_pairs={{0,4},{1,3},{2,6},{3,1},{4,0},{5,7},{6,2},{7,5},{8,12},{9,11},{10,... | collective-permute-start | bytes 2211848 | tf_op jit(solution)/shard_map/ppermute | solution.py:263
  117.5 33.6 %collective-permute-start.17 = (bf16[2,64,2880]{2,1,0:T(8,128)(2,1)S(1)}, bf16[2,64,2880]{2,1,0:T(8,128)(2,1)S(1)}, u32[]{:S(2)}, u32[]{:S(2)}) collective-permute-start(bf16[2,64,2880]{2,1,0:T(8,128)(2,1)S(1)} %copy-done.65), channel_id=1, source_target_pairs={{0,4},{1,3},{2,6},{3,1},{4,0},{5,7},{6,2},{7,5},{8,12},{9,11},{10,... | collective-permute-start | bytes 2211848 | tf_op jit(solution)/shard_map/ppermute | solution.py:263
  118.7 33.0 %collective-permute-start.20 = (bf16[2896,128]{1,0:T(8,128)(2,1)S(1)}, bf16[2896,128]{1,0:T(8,128)(2,1)S(1)}, u32[]{:S(2)}, u32[]{:S(2)}) collective-permute-start(bf16[2896,128]{1,0:T(8,128)(2,1)S(1)} %collective-permute-done.19.own_info.own_ref), channel_id=1, source_target_pairs={{0,2},{1,5},{2,0},{3,7},{4,6},{5,1},{6,4},{7,3},{8,10},{9,13},{10,... | collective-permute-start | bytes 2224136 | tf_op jit(solution)/shard_map/ppermute | solution.py:259
  161.3 15.5 %collective-permute-start.21 = (bf16[2,64,2880]{2,1,0:T(8,128)(2,1)}, bf16[2,64,2880]{2,1,0:T(8,128)(2,1)S(1)}, u32[]{:S(2)}, u32[]{:S(2)}) collective-permute-start(bf16[2,64,2880]{2,1,0:T(8,128)(2,1)} %get-tuple-element.96), channel_id=1, source_target_pairs={{0,4},{1,3},{2,6},{3,1},{4,0},{5,7},{6,2},{7,5},{8,12},{9,11},{10,... | collective-permute-start | bytes 2211848 | tf_op jit(solution)/shard_map/ppermute | solution.py:263
  162.5 15.6 %collective-permute-start.45 = (bf16[2,64,2880]{2,1,0:T(8,128)(2,1)S(1)}, bf16[2,64,2880]{2,1,0:T(8,128)(2,1)S(1)}, u32[]{:S(2)}, u32[]{:S(2)}) collective-permute-start(bf16[2,64,2880]{2,1,0:T(8,128)(2,1)S(1)} %copy-done.64), channel_id=1, source_target_pairs={{0,1},{1,0},{2,3},{3,2},{4,5},{5,4},{6,7},{7,6},{8,9},{9,8},{10,11... | collective-permute-start | bytes 2211848 | tf_op jit(solution)/shard_map/ppermute | solution.py:255
  162.7 22.2 %collective-permute-start.34 = (bf16[2,64,2880]{2,1,0:T(8,128)(2,1)S(1)}, bf16[2,64,2880]{2,1,0:T(8,128)(2,1)S(1)}, u32[]{:S(2)}, u32[]{:S(2)}) collective-permute-start(bf16[2,64,2880]{2,1,0:T(8,128)(2,1)S(1)} %pad_maximum_fusion.11), channel_id=1, source_target_pairs={{0,4},{1,3},{2,6},{3,1},{4,0},{5,7},{6,2},{7,5},{8,12},{9,11},{10,... | collective-permute-start | bytes 2211848 | tf_op jit(solution)/shard_map/ppermute | solution.py:263
  164.8 32.4 %collective-permute-start.26 = (bf16[2,64,2880]{2,1,0:T(8,128)(2,1)S(1)}, bf16[2,64,2880]{2,1,0:T(8,128)(2,1)}, u32[]{:S(2)}, u32[]{:S(2)}) collective-permute-start(bf16[2,64,2880]{2,1,0:T(8,128)(2,1)S(1)} %pad_maximum_fusion.7), channel_id=1, source_target_pairs={{0,1},{1,0},{2,3},{3,2},{4,5},{5,4},{6,7},{7,6},{8,9},{9,8},{10,11... | collective-permute-start | bytes 2211848 | tf_op jit(solution)/shard_map/ppermute | solution.py:255
  168.7 29.7 %collective-permute-start.18 = (bf16[2,64,2880]{2,1,0:T(8,128)(2,1)S(1)}, bf16[2,64,2880]{2,1,0:T(8,128)(2,1)}, u32[]{:S(2)}, u32[]{:S(2)}) collective-permute-start(bf16[2,64,2880]{2,1,0:T(8,128)(2,1)S(1)} %pad_maximum_fusion.5), channel_id=1, source_target_pairs={{0,1},{1,0},{2,3},{3,2},{4,5},{5,4},{6,7},{7,6},{8,9},{9,8},{10,11... | collective-permute-start | bytes 2211848 | tf_op jit(solution)/shard_map/ppermute | solution.py:255
  176.8 16.1 %collective-permute-start.49 = (bf16[2,64,2880]{2,1,0:T(8,128)(2,1)}, bf16[2,64,2880]{2,1,0:T(8,128)(2,1)S(1)}, u32[]{:S(2)}, u32[]{:S(2)}) collective-permute-start(bf16[2,64,2880]{2,1,0:T(8,128)(2,1)} %pad_maximum_fusion.15), channel_id=1, source_target_pairs={{0,4},{1,3},{2,6},{3,1},{4,0},{5,7},{6,2},{7,5},{8,12},{9,11},{10,... | collective-permute-start | bytes 2211848 | tf_op jit(solution)/shard_map/ppermute | solution.py:263
  178.1 20.3 %collective-permute-start.30 = (bf16[2,64,2880]{2,1,0:T(8,128)(2,1)S(1)}, bf16[2,64,2880]{2,1,0:T(8,128)(2,1)}, u32[]{:S(2)}, u32[]{:S(2)}) collective-permute-start(bf16[2,64,2880]{2,1,0:T(8,128)(2,1)S(1)} %pad_maximum_fusion.8), channel_id=1, source_target_pairs={{0,1},{1,0},{2,3},{3,2},{4,5},{5,4},{6,7},{7,6},{8,9},{9,8},{10,11... | collective-permute-start | bytes 2211848 | tf_op jit(solution)/shard_map/ppermute | solution.py:255
  192.9 37.0 %collective-permute-start.41 = (bf16[2880,128]{1,0:T(8,128)(2,1)}, bf16[2880,128]{1,0:T(8,128)(2,1)}, u32[]{:S(2)}, u32[]{:S(2)}) collective-permute-start(bf16[2880,128]{1,0:T(8,128)(2,1)} %get-tuple-element.123), channel_id=1, source_target_pairs={{0,2},{1,5},{2,0},{3,7},{4,6},{5,1},{6,4},{7,3},{8,10},{9,13},{10,... | collective-permute-start | bytes 2211848 | tf_op jit(solution)/shard_map/ppermute | solution.py:259
  197.2 35.8 %collective-permute-start.56 = (bf16[2880,128]{1,0:T(8,128)(2,1)}, bf16[2880,128]{1,0:T(8,128)(2,1)}, u32[]{:S(2)}, u32[]{:S(2)}) collective-permute-start(bf16[2880,128]{1,0:T(8,128)(2,1)} %get-tuple-element.146), channel_id=1, source_target_pairs={{0,2},{1,5},{2,0},{3,7},{4,6},{5,1},{6,4},{7,3},{8,10},{9,13},{10,... | collective-permute-start | bytes 2211848 | tf_op jit(solution)/shard_map/ppermute | solution.py:259
  229.8 21.9 %collective-permute-start.46 = (bf16[2,64,2880]{2,1,0:T(8,128)(2,1)}, bf16[2,64,2880]{2,1,0:T(8,128)(2,1)S(1)}, u32[]{:S(2)}, u32[]{:S(2)}) collective-permute-start(bf16[2,64,2880]{2,1,0:T(8,128)(2,1)} %get-tuple-element.128), channel_id=1, source_target_pairs={{0,1},{1,0},{2,3},{3,2},{4,5},{5,4},{6,7},{7,6},{8,9},{9,8},{10,11... | collective-permute-start | bytes 2211848 | tf_op jit(solution)/shard_map/ppermute | solution.py:255
  232.8 25.6 %collective-permute-start.42 = (bf16[2880,128]{1,0:T(8,128)(2,1)}, bf16[2880,128]{1,0:T(8,128)(2,1)}, u32[]{:S(2)}, u32[]{:S(2)}) collective-permute-start(bf16[2880,128]{1,0:T(8,128)(2,1)} %add_convert_fusion.7), channel_id=1, source_target_pairs={{0,8},{1,9},{2,10},{3,11},{4,12},{5,13},{6,14},{7,15},{8,16},{9,17... | collective-permute-start | bytes 2211848 | tf_op jit(solution)/shard_map/ppermute | solution.py:267
  236.4 43.7 %collective-permute-start.57 = (bf16[2880,128]{1,0:T(8,128)(2,1)}, bf16[2880,128]{1,0:T(8,128)(2,1)S(1)}, u32[]{:S(2)}, u32[]{:S(2)}) collective-permute-start(bf16[2880,128]{1,0:T(8,128)(2,1)} %add_convert_fusion.3), channel_id=1, source_target_pairs={{0,8},{1,9},{2,10},{3,11},{4,12},{5,13},{6,14},{7,15},{8,16},{9,17... | collective-permute-start | bytes 2211848 | tf_op jit(solution)/shard_map/ppermute | solution.py:267
  236.6 16.3 %collective-permute-start.50 = (bf16[2,64,2880]{2,1,0:T(8,128)(2,1)S(1)}, bf16[2,64,2880]{2,1,0:T(8,128)(2,1)S(1)}, u32[]{:S(2)}, u32[]{:S(2)}) collective-permute-start(bf16[2,64,2880]{2,1,0:T(8,128)(2,1)S(1)} %pad_maximum_fusion.14), channel_id=1, source_target_pairs={{0,4},{1,3},{2,6},{3,1},{4,0},{5,7},{6,2},{7,5},{8,12},{9,11},{10,... | collective-permute-start | bytes 2211848 | tf_op jit(solution)/shard_map/ppermute | solution.py:263
  250.7 19.7 %collective-permute-start.40 = (bf16[2880,128]{1,0:T(8,128)(2,1)}, bf16[2880,128]{1,0:T(8,128)(2,1)}, u32[]{:S(2)}, u32[]{:S(2)}) collective-permute-start(bf16[2880,128]{1,0:T(8,128)(2,1)} %get-tuple-element.120), channel_id=1, source_target_pairs={{0,2},{1,5},{2,0},{3,7},{4,6},{5,1},{6,4},{7,3},{8,10},{9,13},{10,... | collective-permute-start | bytes 2211848 | tf_op jit(solution)/shard_map/ppermute | solution.py:259
  251.8 21.1 %collective-permute-start.36 = (bf16[2,64,2880]{2,1,0:T(8,128)(2,1)S(1)}, bf16[2,64,2880]{2,1,0:T(8,128)(2,1)S(1)}, u32[]{:S(2)}, u32[]{:S(2)}) collective-permute-start(bf16[2,64,2880]{2,1,0:T(8,128)(2,1)S(1)} %pad_maximum_fusion.9), channel_id=1, source_target_pairs={{0,4},{1,3},{2,6},{3,1},{4,0},{5,7},{6,2},{7,5},{8,12},{9,11},{10,... | collective-permute-start | bytes 2211848 | tf_op jit(solution)/shard_map/ppermute | solution.py:263
  257.3 28.8 %collective-permute-start.55 = (bf16[2880,128]{1,0:T(8,128)(2,1)}, bf16[2880,128]{1,0:T(8,128)(2,1)S(1)}, u32[]{:S(2)}, u32[]{:S(2)}) collective-permute-start(bf16[2880,128]{1,0:T(8,128)(2,1)} %get-tuple-element.143), channel_id=1, source_target_pairs={{0,2},{1,5},{2,0},{3,7},{4,6},{5,1},{6,4},{7,3},{8,10},{9,13},{10,... | collective-permute-start | bytes 2211848 | tf_op jit(solution)/shard_map/ppermute | solution.py:259
  258.5 30.3 %collective-permute-start.51 = (bf16[2,64,2880]{2,1,0:T(8,128)(2,1)S(1)}, bf16[2,64,2880]{2,1,0:T(8,128)(2,1)S(1)}, u32[]{:S(2)}, u32[]{:S(2)}) collective-permute-start(bf16[2,64,2880]{2,1,0:T(8,128)(2,1)S(1)} %pad_maximum_fusion.13), channel_id=1, source_target_pairs={{0,4},{1,3},{2,6},{3,1},{4,0},{5,7},{6,2},{7,5},{8,12},{9,11},{10,... | collective-permute-start | bytes 2211848 | tf_op jit(solution)/shard_map/ppermute | solution.py:263
  272.8 21.4 %collective-permute-start.43 = (bf16[2880,128]{1,0:T(8,128)(2,1)}, bf16[2880,128]{1,0:T(8,128)(2,1)}, u32[]{:S(2)}, u32[]{:S(2)}) collective-permute-start(bf16[2880,128]{1,0:T(8,128)(2,1)} %add_convert_fusion.6), channel_id=1, source_target_pairs={{0,8},{1,9},{2,10},{3,11},{4,12},{5,13},{6,14},{7,15},{8,16},{9,17... | collective-permute-start | bytes 2211848 | tf_op jit(solution)/shard_map/ppermute | solution.py:267
  279.0 23.0 %collective-permute-start.39 = (bf16[2880,128]{1,0:T(8,128)(2,1)}, bf16[2880,128]{1,0:T(8,128)(2,1)}, u32[]{:S(2)}, u32[]{:S(2)}) collective-permute-start(bf16[2880,128]{1,0:T(8,128)(2,1)} %get-tuple-element.117), channel_id=1, source_target_pairs={{0,2},{1,5},{2,0},{3,7},{4,6},{5,1},{6,4},{7,3},{8,10},{9,13},{10,... | collective-permute-start | bytes 2211848 | tf_op jit(solution)/shard_map/ppermute | solution.py:259
  280.1 23.9 %collective-permute-start.37 = (bf16[2,64,2880]{2,1,0:T(8,128)(2,1)S(1)}, bf16[2,64,2880]{2,1,0:T(8,128)(2,1)S(1)}, u32[]{:S(2)}, u32[]{:S(2)}) collective-permute-start(bf16[2,64,2880]{2,1,0:T(8,128)(2,1)S(1)} %pad_maximum_fusion.4), channel_id=1, source_target_pairs={{0,4},{1,3},{2,6},{3,1},{4,0},{5,7},{6,2},{7,5},{8,12},{9,11},{10,... | collective-permute-start | bytes 2211848 | tf_op jit(solution)/shard_map/ppermute | solution.py:263
  288.3 23.5 %collective-permute-start.58 = (bf16[2880,128]{1,0:T(8,128)(2,1)S(1)}, bf16[2880,128]{1,0:T(8,128)(2,1)S(1)}, u32[]{:S(2)}, u32[]{:S(2)}) collective-permute-start(bf16[2880,128]{1,0:T(8,128)(2,1)S(1)} %add_convert_fusion.2), channel_id=1, source_target_pairs={{0,8},{1,9},{2,10},{3,11},{4,12},{5,13},{6,14},{7,15},{8,16},{9,17... | collective-permute-start | bytes 2211848 | tf_op jit(solution)/shard_map/ppermute | solution.py:267
  293.1 24.5 %collective-permute-start.54 = (bf16[2880,128]{1,0:T(8,128)(2,1)}, bf16[2880,128]{1,0:T(8,128)(2,1)S(1)}, u32[]{:S(2)}, u32[]{:S(2)}) collective-permute-start(bf16[2880,128]{1,0:T(8,128)(2,1)} %get-tuple-element.140), channel_id=1, source_target_pairs={{0,2},{1,5},{2,0},{3,7},{4,6},{5,1},{6,4},{7,3},{8,10},{9,13},{10,... | collective-permute-start | bytes 2211848 | tf_op jit(solution)/shard_map/ppermute | solution.py:259
  294.3 27.3 %collective-permute-start.52 = (bf16[2,64,2880]{2,1,0:T(8,128)(2,1)S(1)}, bf16[2,64,2880]{2,1,0:T(8,128)(2,1)S(1)}, u32[]{:S(2)}, u32[]{:S(2)}) collective-permute-start(bf16[2,64,2880]{2,1,0:T(8,128)(2,1)S(1)} %pad_maximum_fusion.12), channel_id=1, source_target_pairs={{0,4},{1,3},{2,6},{3,1},{4,0},{5,7},{6,2},{7,5},{8,12},{9,11},{10,... | collective-permute-start | bytes 2211848 | tf_op jit(solution)/shard_map/ppermute | solution.py:263
  303.5 27.3 %collective-permute-start.44 = (bf16[2880,128]{1,0:T(8,128)(2,1)S(1)}, bf16[2880,128]{1,0:T(8,128)(2,1)S(1)}, u32[]{:S(2)}, u32[]{:S(2)}) collective-permute-start(bf16[2880,128]{1,0:T(8,128)(2,1)S(1)} %add_convert_fusion.5), channel_id=1, source_target_pairs={{0,8},{1,9},{2,10},{3,11},{4,12},{5,13},{6,14},{7,15},{8,16},{9,17... | collective-permute-start | bytes 2211848 | tf_op jit(solution)/shard_map/ppermute | solution.py:267
  311.8 19.1 %collective-permute-start.38 = (bf16[2880,128]{1,0:T(8,128)(2,1)}, bf16[2880,128]{1,0:T(8,128)(2,1)S(1)}, u32[]{:S(2)}, u32[]{:S(2)}) collective-permute-start(bf16[2880,128]{1,0:T(8,128)(2,1)} %get-tuple-element.114), channel_id=1, source_target_pairs={{0,2},{1,5},{2,0},{3,7},{4,6},{5,1},{6,4},{7,3},{8,10},{9,13},{10,... | collective-permute-start | bytes 2211848 | tf_op jit(solution)/shard_map/ppermute | solution.py:259
  325.9 16.7 %collective-permute-start.59 = (bf16[2880,128]{1,0:T(8,128)(2,1)S(1)}, bf16[2880,128]{1,0:T(8,128)(2,1)S(1)}, u32[]{:S(2)}, u32[]{:S(2)}) collective-permute-start(bf16[2880,128]{1,0:T(8,128)(2,1)S(1)} %add_convert_fusion.1), channel_id=1, source_target_pairs={{0,8},{1,9},{2,10},{3,11},{4,12},{5,13},{6,14},{7,15},{8,16},{9,17... | collective-permute-start | bytes 2211848 | tf_op jit(solution)/shard_map/ppermute | solution.py:267
  (84 other events, 660.6 us)
